TPU v7x, 512 devices: a whole 4x4x16 slice. The times are simulated.
512 devices in a mesh: exp: 64 (over z, x), patch: 8 (over y, core).
Axes of the slice: x: 4, y: 4, z: 16, core: 2. Of those that a mesh axis runs over, the one named last changes fastest.
Arguments:
- image: float32 [64, 1024, 512], P('exp', 'patch'), may hold values from -8 to 8
- row_taps: float32 [20, 41], replicated, may hold values from -1 to 1
- col_taps: float32 [20, 41], replicated, may hold values from -1 to 1
- coefficients: float32 [64, 20], P('exp'), may hold values from -1.5 to 1.5
- exposure_weight: float32 [64], P('exp'), may hold values from 0.25 to 4
- warp_offset: int32 [64, 8, 32], P('exp', 'patch'), may hold values from 0 to 16
- target_cell: int32 [64, 8, 32, 1], P('exp', 'patch'), may hold values from 0 to 63, as said below
Outputs:
- coadd: float32 [8, 64, 16, 128], P('patch', 'exp')
Inputs may be any that keep to these rules, and one draw needn't show every extreme that they name: `target_cell`: no exposure sends more than 2 of its tiles on one patch to one cell, and each exposure sends exactly 2 to some cell of every patch; on every patch one cell receives exactly 2 tiles from every exposure, and every cell receives at least one tile.
All inputs are finite; a program needn't handle non-finite values.
Results may differ from a plain program's by a relative error of at most 0.00012.
Values sent between devices are 32-bit elements; how exact they have to be, the bound alone decides.
A program may use at most 64 MiB of HBM per device.

v0:
```python
import jax
import jax.numpy as jnp
from jax import lax
from jax.sharding import PartitionSpec as P

TR = 16
TW = 128
SHIFT = 8


def extended(cells, sides, width):
    for axis, dim in sides:
        count = lax.axis_size(axis)
        ends = count - 1
        head = lax.slice_in_dim(cells, 0, width, axis=dim)
        tail = lax.slice_in_dim(cells, cells.shape[dim] - width, cells.shape[dim], axis=dim)
        cells = jnp.concatenate(
            [
                lax.ppermute(tail, axis, [(i, (i + 1) % count) for i in range(ends)]),
                cells,
                lax.ppermute(head, axis, [((i + 1) % count, i) for i in range(ends)]),
            ],
            axis=dim,
        )
    return cells


def tap_table(taps, inner, outer):
    ntaps = taps.shape[1]
    differ = jnp.arange(outer)[:, None] - jnp.arange(inner)[None, :]
    onehot = (differ[:, :, None] == jnp.arange(ntaps)[None, None, :]).astype(jnp.float32)
    return jnp.einsum("mxk,bk->mbx", onehot, taps, precision=lax.Precision.HIGHEST)


def per_device(image, row_taps, col_taps, coefficients, exposure_weight, warp_offset, target_cell):
    band_rows = image[0]
    nrows, ncols = band_rows.shape
    radius = row_taps.shape[1] // 2
    tile_rows = TR
    tile_cols = TW
    haloed = extended(band_rows, (("patch", 0),), radius)
    haloed = jnp.pad(haloed, ((0, 0), (radius, radius)))
    horiz_table = tap_table(row_taps, tile_cols, tile_cols + 2 * radius)
    vert_table = tap_table(col_taps, nrows, nrows + 2 * radius) * coefficients[0][None, :, None]
    nblocks = ncols // tile_cols

    def one_block(index):
        window = lax.dynamic_slice_in_dim(haloed, index * tile_cols, tile_cols + 2 * radius, 1)
        spread = jnp.einsum("nm,mbx->nbx", window, horiz_table, precision=lax.Precision.HIGHEST)
        return jnp.einsum("nby,nbx->yx", vert_table, spread, precision=lax.Precision.HIGHEST)

    blocks = lax.map(one_block, jnp.arange(nblocks, dtype=jnp.int32))
    matched = jnp.transpose(blocks, (1, 0, 2)).reshape(nrows, ncols)
    shifted = jnp.pad(matched, ((0, 0), (SHIFT, SHIFT)))
    ntiles = warp_offset.shape[2]
    tile_ids = jnp.arange(ntiles, dtype=jnp.int32)
    row_start = tile_ids // nblocks * tile_rows
    col_start = tile_ids % nblocks * tile_cols + warp_offset[0, 0]

    def cut(row0, col0):
        return lax.dynamic_slice(shifted, (row0, col0), (tile_rows, tile_cols))

    weight_now = exposure_weight[0]
    tiles = jax.vmap(cut)(row_start, col_start).reshape(ntiles, tile_rows * tile_cols) * weight_now
    cells = target_cell[0, 0, :, 0]
    owners = lax.axis_size("exp")
    capacity = max(2, 2 * ((ntiles + owners - 1) // owners))
    earlier = (cells[:, None] == cells[None, :]) & (tile_ids[None, :] < tile_ids[:, None])
    slot_rank = jnp.sum(earlier.astype(jnp.int32), axis=1)
    place = cells * capacity + slot_rank
    routing = (jnp.arange(owners * capacity, dtype=jnp.int32)[:, None] == place[None, :]).astype(
        jnp.float32
    )
    send_tiles = jnp.dot(routing, tiles, precision=lax.Precision.HIGHEST).reshape(
        owners, capacity, tile_rows, tile_cols
    )
    send_weights = (jnp.sum(routing, axis=1) * weight_now).reshape(owners, capacity)
    got_tiles, got_weights = (
        lax.all_to_all(send_tiles, "exp", split_axis=0, concat_axis=0, tiled=True),
        lax.all_to_all(send_weights, "exp", split_axis=0, concat_axis=0, tiled=True),
    )
    numer = jnp.sum(got_tiles, axis=(0, 1))
    denom = jnp.sum(got_weights)
    return (numer / denom)[None, None, :, :]


def solution(mesh):
    return jax.shard_map(
        per_device,
        mesh=mesh,
        in_specs=(
            P("exp", "patch", None),
            P(),
            P(),
            P("exp", None),
            P("exp"),
            P("exp", "patch", None),
            P("exp", "patch", None, None),
        ),
        out_specs=P("patch", "exp", None, None),
        check_vma=False,
    )
```

profile of v0, /device:TPU:1, one launch (start us, length us, event | category | flops | bytes accessed | tf_op | source)
XLA Modules:
  0.0 231.9 jit_solution(8480710195844960743)
XLA Ops:
  1.5 4.6 %collective-permute-start = (f32[20,512]{1,0:T(8,128)}, f32[20,512]{1,0:T(8,128)S(1)}, u32[]{:S(2)}, u32[]{:S(2)}) collective-permute-start(f32[20,512]{1,0:T(8,128)} %get-tuple-element.92), channel_id=1, source_target_pairs={{0,1},{1,2},{2,3},{3,4},{4,5},{5,6},{6,7},{8,9},{9,10},{10,11},{11... | collective-permute-start | bytes 122888 | tf_op jit(solution)/shard_map/ppermute | solution.py:19
  6.1 5.5 %collective-permute-start.1 = (f32[20,512]{1,0:T(8,128)}, f32[20,512]{1,0:T(8,128)}, u32[]{:S(2)}, u32[]{:S(2)}) collective-permute-start(f32[20,512]{1,0:T(8,128)} %get-tuple-element.93), channel_id=1, source_target_pairs={{1,0},{2,1},{3,2},{4,3},{5,4},{6,5},{7,6},{9,8},{10,9},{11,10},{12... | collective-permute-start | bytes 122888 | tf_op jit(solution)/shard_map/ppermute | solution.py:21
  14.7 14.7 %all-to-all-start.1 = ((f32[64,1,2]{2,1,0:T(1,128)}), f32[64,1,2]{2,1,0:T(1,128)S(1)}, u32[]{:S(2)}, u32[]{:S(2)}) async-start(f32[64,1,2]{2,1,0:T(1,128)} %bitcast.22), calls=%async_computation.1 | async-start | bytes 65536 | tf_op jit(solution)/shard_map/all_to_all | solution.py:80
  30.1 2.9 %fusion.9 = f32[168,20,128]{2,1,0:T(8,128)} fusion(s32[168,128]{1,0:T(8,128)S(1)} %iota_subtract_fusion, f32[20,41]{1,0:T(8,128)S(1)} %copy-done), kind=kOutput, calls=%fused_computation.14 | convolution fusion | flops 212481024 | bytes 1809616 | tf_op jit(solution)/shard_map/mxk,bk->mbx/dot_general | solution.py:32
  33.0 2.9 %multiply_bitcast_fusion = f32[168,20,128]{2,1,0:T(8,128)} fusion(s32[168,128]{1,0:T(8,128)S(1)} %iota_subtract_fusion, f32[20]{0:T(128)S(1)} %bitcast.89, f32[20,41]{1,0:T(8,128)S(1)} %copy-done.3), kind=kOutput, calls=%fused_computation.11 | convolution fusion | flops 212911104 | bytes 1809696 | tf_op jit(solution)/shard_map/mxk,bk->mbx/dot_general | solution.py:32
  35.9 2.1 copy.19
  40.8 30.4 %while.11 = (s32[]{:T(128)}, f32[4,128,128]{1,2,0:T(8,128)}, s32[4]{0:T(128)S(1)}, f32[168,552]{1,0:T(8,128)}, f32[168,20,128]{2,0,1:T(8,128)S(1)}, /*index=5*/f...) while((s32[]{:T(128)}, f32[4,128,128]{1,2,0:T(8,128)}, s32[4]{0:T(128)S(1)}, ...), condition=%wide.region_2.3_spmd, body=%wide.region_1.2_spmd.sunk | while | flops 1527644160 | bytes 7119523 | solution.py:52
  42.1 2.6 %fusion.38 = f32[168,20,128]{2,0,1:T(8,128)S(1)} fusion(f32[168,20,128]{2,0,1:T(8,128)S(1)} %get-tuple-element.186, f32[168,552]{1,0:T(8,128)} %get-tuple-element.185, s32[]{:T(128)S(6)} %select_n.68), kind=kOutput, calls=%fused_computation.2.clone.1 | convolution fusion | flops 867041280 | bytes 3612676 | tf_op jit(solution)/shard_map/while/body/eval_jaxpr/nm,mbx->nbx/dot_general | solution.py:49
  44.8 3.7 %fusion.39 = f32[4,128,128]{1,2,0:T(8,128)} fusion(f32[4,128,128]{1,2,0:T(8,128)} %get-tuple-element.173, s32[]{:T(128)} %get-tuple-element.172, f32[168,20,128]{2,0,1:T(8,128)S(1)} %fusion.38, f32[168,20,128]{2,0,1:T(8,128)S(1)} %get-tuple-element.187), kind=kOutput, calls=%fused_computation.1.clone.1 | convolution fusion | flops 660602880 | bytes 3506688 | tf_op jit(solution)/shard_map/while/body/eval_jaxpr/nby,nbx->yx/dot_general | solution.py:50
  49.7 2.6 %fusion.38 = f32[168,20,128]{2,0,1:T(8,128)S(1)} fusion(f32[168,20,128]{2,0,1:T(8,128)S(1)} %get-tuple-element.186, f32[168,552]{1,0:T(8,128)} %get-tuple-element.185, s32[]{:T(128)S(6)} %select_n.68), kind=kOutput, calls=%fused_computation.2.clone.1 | convolution fusion | flops 867041280 | bytes 3612676 | tf_op jit(solution)/shard_map/while/body/eval_jaxpr/nm,mbx->nbx/dot_general | solution.py:49
  52.4 3.7 %fusion.39 = f32[4,128,128]{1,2,0:T(8,128)} fusion(f32[4,128,128]{1,2,0:T(8,128)} %get-tuple-element.173, s32[]{:T(128)} %get-tuple-element.172, f32[168,20,128]{2,0,1:T(8,128)S(1)} %fusion.38, f32[168,20,128]{2,0,1:T(8,128)S(1)} %get-tuple-element.187), kind=kOutput, calls=%fused_computation.1.clone.1 | convolution fusion | flops 660602880 | bytes 3506688 | tf_op jit(solution)/shard_map/while/body/eval_jaxpr/nby,nbx->yx/dot_general | solution.py:50
  57.3 2.6 %fusion.38 = f32[168,20,128]{2,0,1:T(8,128)S(1)} fusion(f32[168,20,128]{2,0,1:T(8,128)S(1)} %get-tuple-element.186, f32[168,552]{1,0:T(8,128)} %get-tuple-element.185, s32[]{:T(128)S(6)} %select_n.68), kind=kOutput, calls=%fused_computation.2.clone.1 | convolution fusion | flops 867041280 | bytes 3612676 | tf_op jit(solution)/shard_map/while/body/eval_jaxpr/nm,mbx->nbx/dot_general | solution.py:49
  60.0 3.7 %fusion.39 = f32[4,128,128]{1,2,0:T(8,128)} fusion(f32[4,128,128]{1,2,0:T(8,128)} %get-tuple-element.173, s32[]{:T(128)} %get-tuple-element.172, f32[168,20,128]{2,0,1:T(8,128)S(1)} %fusion.38, f32[168,20,128]{2,0,1:T(8,128)S(1)} %get-tuple-element.187), kind=kOutput, calls=%fused_computation.1.clone.1 | convolution fusion | flops 660602880 | bytes 3506688 | tf_op jit(solution)/shard_map/while/body/eval_jaxpr/nby,nbx->yx/dot_general | solution.py:50
  64.9 2.6 %fusion.38 = f32[168,20,128]{2,0,1:T(8,128)S(1)} fusion(f32[168,20,128]{2,0,1:T(8,128)S(1)} %get-tuple-element.186, f32[168,552]{1,0:T(8,128)} %get-tuple-element.185, s32[]{:T(128)S(6)} %select_n.68), kind=kOutput, calls=%fused_computation.2.clone.1 | convolution fusion | flops 867041280 | bytes 3612676 | tf_op jit(solution)/shard_map/while/body/eval_jaxpr/nm,mbx->nbx/dot_general | solution.py:49
  67.5 3.7 %fusion.39 = f32[4,128,128]{1,2,0:T(8,128)} fusion(f32[4,128,128]{1,2,0:T(8,128)} %get-tuple-element.173, s32[]{:T(128)} %get-tuple-element.172, f32[168,20,128]{2,0,1:T(8,128)S(1)} %fusion.38, f32[168,20,128]{2,0,1:T(8,128)S(1)} %get-tuple-element.187), kind=kOutput, calls=%fused_computation.1.clone.1 | convolution fusion | flops 660602880 | bytes 3506688 | tf_op jit(solution)/shard_map/while/body/eval_jaxpr/nby,nbx->yx/dot_general | solution.py:50
  72.5 85.4 %while.12 = (s32[]{:T(128)}, f32[128,528]{1,0:T(8,128)S(1)}, s32[32,2]{0,1:T(2,128)S(1)}, f32[32,16,128]{2,1,0:T(8,128)}, s32[]{:T(128)}) while((s32[]{:T(128)}, f32[128,528]{1,0:T(8,128)S(1)}, s32[32,2]{0,1:T(2,128)S(1)}, f32[32,16,128]{2,1,0:T(8,128)}, s32[]{:T(128)}) %tuple.41), condition=%wide.while_cond, body=%wide.while_body.sunk | while | flops 2 | bytes 18017 | solution.py:61
  75.8 2.0 bitcast_dynamic-update-slice_fusion.2
  78.5 2.0 bitcast_dynamic-update-slice_fusion.2
  81.2 2.0 bitcast_dynamic-update-slice_fusion.2
  86.5 2.0 bitcast_dynamic-update-slice_fusion.2
  91.8 2.0 bitcast_dynamic-update-slice_fusion.2
  99.8 2.0 bitcast_dynamic-update-slice_fusion.2
  102.5 2.0 bitcast_dynamic-update-slice_fusion.2
  105.2 2.0 bitcast_dynamic-update-slice_fusion.2
  113.2 2.0 bitcast_dynamic-update-slice_fusion.2
  134.5 2.0 bitcast_dynamic-update-slice_fusion.2
  137.2 2.0 bitcast_dynamic-update-slice_fusion.2
  145.2 2.0 bitcast_dynamic-update-slice_fusion.2
  150.5 2.0 bitcast_dynamic-update-slice_fusion.2
  155.9 2.0 bitcast_dynamic-update-slice_fusion.2
  161.1 14.5 %all-to-all-start = ((f32[64,2,16,128]{3,2,1,0:T(8,128)}), f32[64,2,16,128]{3,2,1,0:T(8,128)S(1)}, u32[]{:S(2)}, u32[]{:S(2)}) async-start(f32[64,2,16,128]{3,2,1,0:T(8,128)} %copy.23), calls=%async_computation | async-start | bytes 2097152 | tf_op jit(solution)/shard_map/all_to_all | solution.py:79
  176.4 54.1 %all-to-all-done = f32[64,2,16,128]{3,2,1,0:T(8,128)S(1)} async-done(((f32[64,2,16,128]{3,2,1,0:T(8,128)}), f32[64,2,16,128]{3,2,1,0:T(8,128)S(1)}, u32[]{:S(2)}, u32[]{:S(2)}) %all-to-all-start) | async-done | bytes 1048608 | tf_op jit(solution)/shard_map/all_to_all | solution.py:79
  (122 shorter events, 74.0 us)
Async XLA Ops:
  0.0 30.1 %copy-start = (f32[20,41]{1,0:T(8,128)S(1)}, f32[20,41]{1,0:T(8,128)}, u32[]{:S(2)}) copy-start(f32[20,41]{1,0:T(8,128)} %param.10) | copy-start | bytes 9844
  0.0 33.0 %copy-start.4 = (f32[1,20]{1,0:T(1,128)S(1)}, f32[1,20]{1,0:T(1,128)}, u32[]{:S(2)}) copy-start(f32[1,20]{1,0:T(1,128)} %param.12) | copy-start | bytes 244
  0.0 33.0 %copy-start.3 = (f32[20,41]{1,0:T(8,128)S(1)}, f32[20,41]{1,0:T(8,128)}, u32[]{:S(2)}) copy-start(f32[20,41]{1,0:T(8,128)} %param.11) | copy-start | bytes 9844
  1.5 37.0 %collective-permute-start = (f32[20,512]{1,0:T(8,128)}, f32[20,512]{1,0:T(8,128)S(1)}, u32[]{:S(2)}, u32[]{:S(2)}) collective-permute-start(f32[20,512]{1,0:T(8,128)} %get-tuple-element.92), channel_id=1, source_target_pairs={{0,1},{1,2},{2,3},{3,4},{4,5},{5,6},{6,7},{8,9},{9,10},{10,11},{11... | collective-permute-start | bytes 122888 | tf_op jit(solution)/shard_map/ppermute | solution.py:19
  6.1 32.4 %collective-permute-start.1 = (f32[20,512]{1,0:T(8,128)}, f32[20,512]{1,0:T(8,128)}, u32[]{:S(2)}, u32[]{:S(2)}) collective-permute-start(f32[20,512]{1,0:T(8,128)} %get-tuple-element.93), channel_id=1, source_target_pairs={{1,0},{2,1},{3,2},{4,3},{5,4},{6,5},{7,6},{9,8},{10,9},{11,10},{12... | collective-permute-start | bytes 122888 | tf_op jit(solution)/shard_map/ppermute | solution.py:21
  14.7 146.4 %all-to-all-start.1 = ((f32[64,1,2]{2,1,0:T(1,128)}), f32[64,1,2]{2,1,0:T(1,128)S(1)}, u32[]{:S(2)}, u32[]{:S(2)}) async-start(f32[64,1,2]{2,1,0:T(1,128)} %bitcast.22), calls=%async_computation.1 | async-start | bytes 65536 | tf_op jit(solution)/shard_map/all_to_all | solution.py:80
  35.9 2.2 copy-start.1
  38.1 0.9 copy-start.2
  161.1 69.4 %all-to-all-start = ((f32[64,2,16,128]{3,2,1,0:T(8,128)}), f32[64,2,16,128]{3,2,1,0:T(8,128)S(1)}, u32[]{:S(2)}, u32[]{:S(2)}) async-start(f32[64,2,16,128]{3,2,1,0:T(8,128)} %copy.23), calls=%async_computation | async-start | bytes 2097152 | tf_op jit(solution)/shard_map/all_to_all | solution.py:79
where the time goes:
time: 233 us; the launch traced here: 232 us
  local copies, waits for them, and re-layouts  96.1 us (41%)
  waiting for transfers between devices  54.1 us (23%)
  starting transfers between devices  39.3 us (17%)
  matrix products  31.7 us (14%)
  other arithmetic  7.25 us (3%)
  loops' own time  2.67 us (1%)
    gather x96, local copies, waits for them, and re-layouts  85.3 us
    all_to_all x1, waiting for transfers between devices, per_device(): lax.all_to_all(send_tiles, 'exp', split_axis=0, concat_axis=0, tiled=True)  54.1 us
    dot_general x4, matrix products, one_block(): jnp.einsum('nby,nbx->yx', vert_table, spread, precision=lax.Precision.HIG...  14.7 us
    all_to_all x1, starting transfers between devices, per_device(): lax.all_to_all(send_weights, 'exp', split_axis=0, concat_axis=0, tiled=True)  14.7 us
    all_to_all x1, starting transfers between devices, per_device(): lax.all_to_all(send_tiles, 'exp', split_axis=0, concat_axis=0, tiled=True)  14.5 us
    dot_general x4, matrix products, one_block(): jnp.einsum('nm,mbx->nbx', window, horiz_table, precision=lax.Precision.HI...  10.5 us
    dot_general x2, matrix products, tap_table(): jnp.einsum('mxk,bk->mbx', onehot, taps, precision=lax.Precision.HIGHEST)  5.81 us
    ppermute x1, starting transfers between devices, extended(): lax.ppermute(head, axis, [((i + 1) % count, i) for i in range(ends)])  5.49 us
  transfers between devices with their start and end apart: 4, of which 1 were waited for; matrix products, arithmetic and copies ran while one was open for 57% of the time, Pallas kernels for 0%

commit v1 on v0

v1 whole, which is shorter than its diff:
```python
import functools

import jax
import jax.numpy as jnp
from jax import lax
from jax.experimental import pallas as pl
from jax.experimental.pallas import tpu as pltpu
from jax.sharding import PartitionSpec as P

NB = 20
TAPS = 41
HALF = 20
NROWS = 128
NCOLS = 512
TR = 16
TW = 128
SHIFT = 8
NTILES = 32
NX = 4
PAD = 24
F32 = jnp.float32
BF16 = jnp.bfloat16
MESH = pl.DeviceIdType.MESH
ROWQ = 4
XB = 64
NJ = NCOLS // XB
NA = (ROWQ + TAPS + ROWQ - 2) // ROWQ
NKAP = NA * ROWQ
NQ = NROWS // ROWQ
NG = 48


def lanes(rows):
    return lax.broadcasted_iota(jnp.int32, (rows, 128), 1)


def build_patterns(coef_ref, row_ref, col_ref, scaled, rhi, rlo):
    for b in range(NB):
        scaled[b : b + 1, :] = col_ref[b : b + 1, :] * coef_ref[0, b]
    tap = lax.broadcasted_iota(jnp.int32, (TAPS, 128), 0)
    place = lax.broadcasted_iota(jnp.int32, (TAPS, 128), 1)
    flip = jnp.where((XB - place % XB) % XB == tap, 1.0, 0.0).astype(F32)
    rowpat = jnp.dot(row_ref[...], flip, precision=lax.Precision.HIGHEST, preferred_element_type=F32)
    pats = lax.dot_general(
        scaled[...], rowpat, (((0,), (0,)), ((), ())), precision=lax.Precision.HIGHEST, preferred_element_type=F32
    )
    gap = lax.broadcasted_iota(jnp.int32, (128, 128), 0) - lanes(128) % XB
    keep = (gap >= 0) & (gap < TAPS)
    for i in range(TAPS):
        base = jnp.broadcast_to(pats[i : i + 1, :], (XB, 128))
        ring = pltpu.roll(base, 0, 1, stride=1, stride_axis=0)
        band = jnp.where(keep, jnp.concatenate([ring, ring], axis=0), 0.0)
        high = band.astype(BF16)
        rhi[i + ROWQ - 1] = high
        rlo[i + ROWQ - 1] = (band - high.astype(F32)).astype(BF16)
    zero = jnp.zeros((128, 128), BF16)
    for i in list(range(ROWQ - 1)) + list(range(TAPS + ROWQ - 1, NKAP + ROWQ - 1)):
        rhi[i] = zero
        rlo[i] = zero


def build_weights(rhi, rlo, whi, wlo):
    left = lanes(128) < XB

    def one(kappa, carry):
        rows = pl.ds(pl.multiple_of(kappa * 128, 128), 128)
        for src, dst in ((rhi, whi), (rlo, wlo)):
            dst[rows, 0:128] = jnp.where(left, src[kappa + 3], src[kappa + 2])
            dst[rows, 128:256] = jnp.where(left, src[kappa + 1], src[kappa])
        return carry

    lax.fori_loop(0, NKAP, one, 0)


def build_planes(buf, phi, plo):
    lane = lanes(NG)

    def one(rho, carry):
        cols = [buf[j, pl.ds(rho, NG, stride=ROWQ), :] for j in range(4)]
        zero = jnp.zeros((NG, 128), F32)
        padded = [zero] + cols + [zero]
        for j in range(4):
            even = jnp.where(lane < HALF, pltpu.roll(padded[j], HALF, 1), pltpu.roll(padded[j + 1], HALF, 1))
            odd = jnp.where(
                lane < XB + HALF, pltpu.roll(padded[j + 1], XB + HALF, 1), pltpu.roll(padded[j + 2], XB + HALF, 1)
            )
            for place, part in ((2 * j, even), (2 * j + 1, odd)):
                high = part.astype(BF16).astype(F32)
                phi[rho, place] = high
                plo[rho, place] = part - high
        return carry

    lax.fori_loop(0, ROWQ, one, 0)


def convolve(phi, plo, whi, wlo, acc):
    total = None
    for a in range(NA):
        def lhs(src):
            return jnp.concatenate(
                [
                    jnp.concatenate([src[rho, j, a + 1 : a + 1 + NQ, :].astype(BF16) for j in range(NJ)], axis=0)
                    for rho in range(ROWQ)
                ],
                axis=1,
            )

        high, low = lhs(phi), lhs(plo)
        rows = slice(a * 512, (a + 1) * 512)
        part = (
            jnp.dot(high, whi[rows, :], preferred_element_type=F32)
            + jnp.dot(low, whi[rows, :], preferred_element_type=F32)
            + jnp.dot(high, wlo[rows, :], preferred_element_type=F32)
        )
        if a == 0:
            acc[...] = part
        else:
            acc[...] += part


def to_matched(acc, mat, weight):
    left = lanes(NQ) < XB
    mat[0] = jnp.zeros((NROWS, 128), F32)
    mat[5] = jnp.zeros((NROWS, 128), F32)
    for j in range(4):
        for pair in range(2):
            cols = slice(pair * 128, pair * 128 + 128)
            even = acc[2 * j * NQ : (2 * j + 1) * NQ, cols] * weight
            odd = acc[(2 * j + 1) * NQ : (2 * j + 2) * NQ, cols] * weight
            mat[j + 1, pl.ds(2 * pair, NQ, stride=ROWQ), :] = jnp.where(left, even, pltpu.roll(odd, XB, 1))
            mat[j + 1, pl.ds(2 * pair + 1, NQ, stride=ROWQ), :] = jnp.where(left, pltpu.roll(even, XB, 1), odd)


def cut_tiles(offs_ref, mat, tiles):
    lane = lanes(TR)
    tiles[NTILES] = jnp.zeros((TR, 128), F32)

    def one(t, carry):
        rows = pl.ds(pl.multiple_of(t * TR, TR), TR)
        for q in range(4):
            off = offs_ref[0, t * 4 + q]
            side = jnp.where(off >= SHIFT, q + 2, q)
            turn = (128 + SHIFT - off) % 128
            own = pltpu.roll(mat[q + 1, rows, :], turn, 1)
            other = pltpu.roll(mat[side, rows, :], turn, 1)
            source = lane + (off - SHIFT)
            tiles[t * 4 + q] = jnp.where((source >= 0) & (source < 128), own, other)
        return carry

    lax.fori_loop(0, NROWS // TR, one, 0)


def gather_cells(slots, tiles, send, cells, h):
    rows = slice(h * 8, h * 8 + 8)

    def one(depth, carry):
        for x in range(NX):
            cell = depth * NX + x
            send[h, x, depth] = tiles[slots[0, cell], rows, :] + tiles[slots[1, cell], rows, :]
        return carry

    lax.fori_loop(0, cells // NX, one, 0)


def kernel(
    nz, npatch,
    offs_ref, cell_ref, coef_ref, wgt_ref, row_ref, col_ref, img_ref, out_ref,
    buf, scaled, rhi, rlo, whi, wlo, phi, plo, acc, mat, tiles,
    slotv, slots, denx, denz, send, recv_far, recv_near, xsum, recv_z,
    load_sem, slot_sem, halo_send, halo_recv, denx_send, denx_recv, denz_send, denz_recv,
    far_send, far_recv, near_send, near_recv, z_send, z_recv,
):
    cells = nz * NX
    half = nz // 2
    me, patch = lax.axis_index("exp"), lax.axis_index("patch")
    zpos, xpos = me // NX, me % NX
    right, left, across = (xpos + 1) % NX, (xpos + NX - 1) % NX, (xpos + 2) % NX
    barrier = pltpu.get_barrier_semaphore()

    def along_x(x):
        return (zpos * NX + x, patch)

    def along_z(d):
        return ((zpos + d) % nz * NX + xpos, patch)

    def load(j):
        return pltpu.make_async_copy(
            img_ref.at[:, pl.ds(j * 128, 128)], buf.at[j, pl.ds(PAD, NROWS), :], load_sem.at[j]
        )

    def halo(way):
        source, target = ((NROWS, 0), (PAD, PAD + NROWS))[way]
        return pltpu.make_async_remote_copy(
            src_ref=buf.at[:, pl.ds(source, PAD), :],
            dst_ref=buf.at[:, pl.ds(target, PAD), :],
            send_sem=halo_send.at[way],
            recv_sem=halo_recv.at[way],
            device_id=(me, patch + (1, -1)[way]),
            device_id_type=MESH,
        )

    def remote(src, dst, ssem, rsem, target):
        return pltpu.make_async_remote_copy(
            src_ref=src, dst_ref=dst, send_sem=ssem, recv_sem=rsem, device_id=target, device_id_type=MESH
        )

    def den_x(n):
        return remote(
            denx.at[0], denx.at[n], denx_send.at[n], denx_recv.at[n], along_x((xpos + n) % NX)
        )

    def den_z(d):
        return remote(denz.at[0], denz.at[d], denz_send.at[d], denz_recv.at[d], along_z(d))

    def far(h, way):
        return remote(
            send.at[h, across, pl.ds(way * half, half)],
            recv_far.at[h, way],
            far_send.at[2 * h + way],
            far_recv.at[2 * h + way],
            along_x((right, left)[way]),
        )

    def near(h, way, part):
        x = (right, left)[way]
        rows = pl.ds(part * half, half)
        place = 4 * h + 2 * way + part
        return remote(
            send.at[h, x, rows], recv_near.at[h, way, rows], near_send.at[place], near_recv.at[place], along_x(x)
        )

    def deep(h, d):
        return remote(
            xsum.at[h, (zpos + d) % nz], recv_z.at[h, d], z_send.at[h, d], z_recv.at[h, d], along_z(d)
        )

    def each(count, action):
        lax.fori_loop(1, count, lambda d, carry: (action(d), carry)[1], 0)

    for j in range(4):
        load(j).start()

    def greet(target):
        pl.semaphore_signal(barrier, inc=1, device_id=target, device_id_type=MESH)

    @pl.when(patch > 0)
    def _():
        greet((me, patch - 1))

    @pl.when(patch < npatch - 1)
    def _():
        greet((me, patch + 1))

    for n in range(1, NX):
        greet(along_x((xpos + n) % NX))
    each(nz, lambda d: greet(along_z(d)))

    lane = lax.broadcasted_iota(jnp.int32, (8, 128), 1)
    first = jnp.full((8, 128), NTILES, jnp.int32)
    last = jnp.full((8, 128), -1, jnp.int32)
    count = jnp.zeros((8, 128), F32)
    for k in range(NTILES):
        hit = lane == cell_ref[0, k]
        count = count + jnp.where(hit, 1.0, 0.0)
        first = jnp.minimum(first, jnp.where(hit, k, NTILES))
        last = jnp.maximum(last, jnp.where(hit, k, -1))
    sub = lax.broadcasted_iota(jnp.int32, (8, 128), 0)
    slotv[...] = jnp.where(sub == 0, first, jnp.where(last > first, last, NTILES))
    slot_copy = pltpu.make_async_copy(slotv, slots, slot_sem)
    slot_copy.start()
    denx[0] = (count * wgt_ref[0])[0:1]

    build_patterns(coef_ref, row_ref, col_ref, scaled, rhi, rlo)

    neighbours = jnp.where(patch > 0, 1, 0) + jnp.where(patch < npatch - 1, 1, 0)
    pl.semaphore_wait(barrier, neighbours + NX - 1 + nz - 1)
    for j in range(4):
        load(j).wait()

    @pl.when(patch < npatch - 1)
    def _():
        halo(0).start()

    @pl.when(patch > 0)
    def _():
        halo(1).start()

    for n in range(1, NX):
        den_x(n).start()

    @pl.when(patch == 0)
    def _():
        buf[:, 0:PAD, :] = jnp.zeros((4, PAD, 128), F32)

    @pl.when(patch == npatch - 1)
    def _():
        buf[:, PAD + NROWS : PAD + NROWS + PAD, :] = jnp.zeros((4, PAD, 128), F32)

    buf[:, PAD + NROWS + PAD :, :] = jnp.zeros((4, NG * ROWQ - NROWS - 2 * PAD, 128), F32)

    build_weights(rhi, rlo, whi, wlo)

    for n in range(1, NX):
        den_x(n).wait_recv()
    denz[0] = denx[0] + denx[1] + denx[2] + denx[3]
    each(nz, lambda d: den_z(d).start())

    @pl.when(patch > 0)
    def _():
        halo(0).wait_recv()

    @pl.when(patch < npatch - 1)
    def _():
        halo(1).wait_recv()

    build_planes(buf, phi, plo)
    convolve(phi, plo, whi, wlo, acc)
    to_matched(acc, mat, wgt_ref[0])
    cut_tiles(offs_ref, mat, tiles)
    slot_copy.wait()
    for h in range(2):
        gather_cells(slots, tiles, send, cells, h)
        for way in range(2):
            far(h, way).start()
        near(h, 0, 1).start()
        near(h, 1, 0).start()

    for h in range(2):
        for way in range(2):
            far(h, way).wait_recv()
            x = (right, left)[way]
            rows = pl.ds(way * half, half)
            send[h, x, rows] += recv_far[h, way]
            near(h, way, way).start()

    for h in range(2):
        for way in range(2):
            for part in range(2):
                near(h, way, part).wait_recv()
        xsum[h] = send[h, xpos] + recv_near[h, 0] + recv_near[h, 1]
        each(nz, lambda d: deep(h, d).start())

    each(nz, lambda d: den_z(d).wait_recv())
    den = denz[0]
    for d in range(1, nz):
        den = den + denz[d]
    den = jnp.sum(jnp.where(lanes(1) == me, den, 0.0), axis=1, keepdims=True)
    for h in range(2):
        def add(d, total):
            deep(h, d).wait_recv()
            return total + recv_z[h, d]

        total = lax.fori_loop(1, nz, add, xsum[h, zpos])
        out_ref[h * 8 : h * 8 + 8, :] = total / den

    @pl.when(patch < npatch - 1)
    def _():
        halo(0).wait_send()

    @pl.when(patch > 0)
    def _():
        halo(1).wait_send()

    for n in range(1, NX):
        den_x(n).wait_send()
    each(nz, lambda d: den_z(d).wait_send())
    for h in range(2):
        for way in range(2):
            far(h, way).wait_send()
            for part in range(2):
                near(h, way, part).wait_send()
        each(nz, lambda d: deep(h, d).wait_send())


def per_device(nz, npatch, image, row_taps, col_taps, coefficients, exposure_weight, warp_offset, target_cell):
    smem = pl.BlockSpec(memory_space=pltpu.SMEM)
    vmem = pl.BlockSpec(memory_space=pltpu.VMEM)
    half = nz // 2
    scratch = pltpu.VMEM
    dma = pltpu.SemaphoreType.DMA
    out = pl.pallas_call(
        functools.partial(kernel, nz, npatch),
        out_shape=jax.ShapeDtypeStruct((TR, TW), F32),
        in_specs=[smem, smem, smem, smem, vmem, vmem, pl.BlockSpec(memory_space=pl.ANY)],
        out_specs=vmem,
        scratch_shapes=[
            scratch((4, NG * ROWQ, 128), F32),
            scratch((NB, TAPS), F32),
            scratch((NKAP + ROWQ - 1, 128, 128), BF16),
            scratch((NKAP + ROWQ - 1, 128, 128), BF16),
            scratch((NKAP * 128, 256), BF16),
            scratch((NKAP * 128, 256), BF16),
            scratch((ROWQ, NJ, NG, 128), F32),
            scratch((ROWQ, NJ, NG, 128), F32),
            scratch((NJ * NQ, 256), F32),
            scratch((6, NROWS, 128), F32),
            scratch((NTILES + 1, TR, TW), F32),
            scratch((8, 128), jnp.int32),
            pltpu.SMEM((8, 128), jnp.int32),
            scratch((NX, 1, 128), F32),
            scratch((nz, 1, 128), F32),
            scratch((2, NX, nz, 8, 128), F32),
            scratch((2, 2, half, 8, 128), F32),
            scratch((2, 2, nz, 8, 128), F32),
            scratch((2, nz, 8, 128), F32),
            scratch((2, nz, 8, 128), F32),
            dma((4,)),
            dma,
            dma((2,)),
            dma((2,)),
            dma((NX,)),
            dma((NX,)),
            dma((nz,)),
            dma((nz,)),
            dma((4,)),
            dma((4,)),
            dma((8,)),
            dma((8,)),
            dma((2, nz)),
            dma((2, nz)),
        ],
        compiler_params=pltpu.CompilerParams(
            collective_id=0, has_side_effects=True, vmem_limit_bytes=48 * 2**20
        ),
    )(
        warp_offset.reshape(1, NTILES),
        target_cell.reshape(1, NTILES),
        coefficients,
        exposure_weight,
        row_taps,
        col_taps,
        image.reshape(NROWS, NCOLS),
    )
    return out[None, None]


def solution(mesh):
    nz = mesh.shape["exp"] // NX
    npatch = mesh.shape["patch"]
    return jax.shard_map(
        functools.partial(per_device, nz, npatch),
        mesh=mesh,
        in_specs=(
            P("exp", "patch", None),
            P(),
            P(),
            P("exp", None),
            P("exp"),
            P("exp", "patch", None),
            P("exp", "patch", None, None),
        ),
        out_specs=P("patch", "exp", None, None),
        check_vma=False,
    )
```

time: 233 us -> 45.4 us (0.19)
  local copies, waits for them, and re-layouts: 96.1 us -> 3.63 us
  waiting for transfers between devices: 54.1 us -> 0 us
  Pallas kernels: 0 us -> 40.9 us
  starting transfers between devices: 39.3 us -> 0 us
  matrix products: 31.7 us -> 0 us
  other arithmetic: 7.25 us -> 0 us
  loops' own time: 2.67 us -> 0 us
    gather x96 -> x0, local copies, waits for them, and re-layouts: 85.3 us -> none
    all_to_all x2 -> x0, waiting for transfers between devices: 54.1 us -> none  [the longest x1 54.1 us: per_device(): lax.all_to_all(send_tiles, 'exp', split_axis=0, concat_axis=0, tiled=True)]
    pallas_call x0 -> x1, Pallas kernels: none -> 40.9 us  [per_device(): pl.pallas_call(functools.partial(kernel, nz, npatch), out_shape=jax.Shape...]
    dot_general x11 -> x0, matrix products: 31.7 us -> none  [the longest x4 14.7 us: one_block(): jnp.einsum('nby,nbx->yx', vert_table, spread, precision=lax.Precision.HIG...]
    all_to_all x2 -> x0, starting transfers between devices: 29.2 us -> none  [the longest x1 14.7 us: per_device(): lax.all_to_all(send_weights, 'exp', split_axis=0, concat_axis=0, tiled=True)]
    ppermute x2 -> x0, starting transfers between devices: 10.1 us -> none  [the longest x1 5.49 us: extended(): lax.ppermute(head, axis, [((i + 1) % count, i) for i in range(ends)])]
    unnamed x10 -> x13, local copies, waits for them, and re-layouts: 0.73 us -> 3.63 us
    another operation x2 -> x0, loops' own time: 2.67 us -> none  [the longest x1 2.61 us: per_device(): blocks = lax.map(one_block, jnp.arange(nblocks, dtype=jnp.int32))]
  transfers between devices with their start and end apart: 4 -> 0, of which waited for: 1 -> 0; matrix products, arithmetic and copies ran while one was open for 57% -> 0% of each run, Pallas kernels for 0% -> 0%
where the time goes in v1:
time: 45.4 us; the launch traced here: 45.2 us
  Pallas kernels  40.9 us (90%)
  local copies, waits for them, and re-layouts  3.63 us (8%)
  between operations  0.69 us (2%)
    pallas_call x1, Pallas kernels, per_device(): pl.pallas_call(functools.partial(kernel, nz, npatch), out_shape=jax.Shape...  40.9 us
    unnamed x13, local copies, waits for them, and re-layouts  3.63 us

profile of v1, /device:TPU:1, one launch (start us, length us, event | category | flops | bytes accessed | tf_op | source)
XLA Modules:
  0.0 45.2 jit_solution(5023190240097759840)
XLA Ops:
  0.7 0.0 copy-start.3
  0.7 0.0 copy-start.4
  0.7 0.0 copy-start.5
  0.7 0.6 %copy-done.3 = s32[1,1,32]{2,1,0:T(1,128)S(1)} copy-done((s32[1,1,32]{2,1,0:T(1,128)S(1)}, s32[1,1,32]{2,1,0:T(1,128)}, u32[]{:S(2)}) %copy-start.3) | copy-done | bytes 152
  1.3 0.0 copy-done.4
  1.3 0.0 copy-done.5
  1.3 0.0 copy-start
  1.3 0.9 %copy-done = f32[1,128,512]{2,1,0:T(8,128)S(1)} copy-done((f32[1,128,512]{2,1,0:T(8,128)S(1)}, f32[1,128,512]{2,1,0:T(8,128)}, u32[]{:S(2)}) %copy-start) | copy-done | bytes 262168
  2.3 0.0 copy-start.1
  2.3 0.7 %copy-done.1 = f32[20,41]{1,0:T(8,128)S(1)} copy-done((f32[20,41]{1,0:T(8,128)S(1)}, f32[20,41]{1,0:T(8,128)}, u32[]{:S(2)}) %copy-start.1) | copy-done | bytes 3304
  3.0 0.0 copy-start.2
  3.0 0.7 %copy-done.2 = f32[20,41]{1,0:T(8,128)S(1)} copy-done((f32[20,41]{1,0:T(8,128)S(1)}, f32[20,41]{1,0:T(8,128)}, u32[]{:S(2)}) %copy-start.2) | copy-done | bytes 3304
  3.7 40.9 %shard_map.73 = f32[16,128]{1,0:T(8,128)S(1)} custom-call(s32[1,32]{1,0:T(1,128)S(1)} %bitcast.6, s32[1,32]{1,0:T(1,128)S(1)} %bitcast.7, f32[1,20]{1,0:T(1,128)S(1)} %copy-done.5, f32[1]{0:T(128)S(6)} %copy.9.wgt_ref, f32[20,41]{1,0:T(8,128)S(1)} %copy-done.1, f32[20,41]{1,0:T(8,128)S(1)} %copy-done.2, f32[128,512]{1,0:T(8,128)S(1)} %bitcast.4), custom_call_target="tpu_custom_call" | custom-call | tf_op jit(solution)/shard_map/pallas_call | solution.py:381
  44.6 0.6 %copy.10 = f32[1,1,16,128]{3,2,1,0:T(8,128)} copy(f32[1,1,16,128]{3,2,1,0:T(8,128)S(1)} %bitcast.5) | data formatting | bytes 16384
Async XLA Ops:
  0.7 0.7 %copy-start.3 = (s32[1,1,32]{2,1,0:T(1,128)S(1)}, s32[1,1,32]{2,1,0:T(1,128)}, u32[]{:S(2)}) copy-start(s32[1,1,32]{2,1,0:T(1,128)} %param.12) | copy-start | bytes 388
  0.7 0.7 %copy-start.4 = (s32[1,1,32,1]{2,3,1,0:T(1,128)S(1)}, s32[1,1,32,1]{2,3,1,0:T(1,128)}, u32[]{:S(2)}) copy-start(s32[1,1,32,1]{2,3,1,0:T(1,128)} %param.13) | copy-start | bytes 388
  0.7 0.7 %copy-start.5 = (f32[1,20]{1,0:T(1,128)S(1)}, f32[1,20]{1,0:T(1,128)}, u32[]{:S(2)}) copy-start(f32[1,20]{1,0:T(1,128)} %coef_ref.1) | copy-start | bytes 244
  1.3 0.9 %copy-start = (f32[1,128,512]{2,1,0:T(8,128)S(1)}, f32[1,128,512]{2,1,0:T(8,128)}, u32[]{:S(2)}) copy-start(f32[1,128,512]{2,1,0:T(8,128)} %param.7) | copy-start | bytes 786436
  2.3 0.7 %copy-start.1 = (f32[20,41]{1,0:T(8,128)S(1)}, f32[20,41]{1,0:T(8,128)}, u32[]{:S(2)}) copy-start(f32[20,41]{1,0:T(8,128)} %row_ref.1) | copy-start | bytes 9844
  3.0 0.7 %copy-start.2 = (f32[20,41]{1,0:T(8,128)S(1)}, f32[20,41]{1,0:T(8,128)}, u32[]{:S(2)}) copy-start(f32[20,41]{1,0:T(8,128)} %col_ref.1) | copy-start | bytes 9844

commit v2 on v1

v2 whole, which is shorter than its diff:
```python
import functools

import jax
import jax.numpy as jnp
from jax import lax
from jax.experimental import pallas as pl
from jax.experimental.pallas import tpu as pltpu
from jax.sharding import PartitionSpec as P

NB = 20
TAPS = 41
HALF = 20
NROWS = 128
NCOLS = 512
TR = 16
TW = 128
SHIFT = 8
NTILES = 32
NX = 4
PAD = 24
F32 = jnp.float32
BF16 = jnp.bfloat16
MESH = pl.DeviceIdType.MESH
ROWQ = 4
XB = 64
NJ = NCOLS // XB
NA = (ROWQ + TAPS + ROWQ - 2) // ROWQ
NKAP = NA * ROWQ
NQ = NROWS // ROWQ
NG = 48
NCHUNK = 4


def lanes(rows):
    return lax.broadcasted_iota(jnp.int32, (rows, 128), 1)


def build_weights(coef_ref, row_ref, col_ref, scaled, phigh, plow):
    for b in range(NB):
        scaled[b : b + 1, :] = col_ref[b : b + 1, :] * coef_ref[0, b]
    tap = lax.broadcasted_iota(jnp.int32, (TAPS, 128), 0)
    place = lax.broadcasted_iota(jnp.int32, (TAPS, 128), 1)
    flip = jnp.where((XB - place % XB) % XB == tap, 1.0, 0.0).astype(F32)
    rowpat = jnp.dot(row_ref[...], flip, precision=lax.Precision.HIGHEST, preferred_element_type=F32)
    pats = lax.dot_general(
        scaled[...], rowpat, (((0,), (0,)), ((), ())), precision=lax.Precision.HIGHEST, preferred_element_type=F32
    )
    left = lanes(XB) < XB
    gap = lax.broadcasted_iota(jnp.int32, (128, 128), 0) - lanes(128) % XB
    keep = (gap >= 0) & (gap < TAPS)
    zero = jnp.zeros((XB, 128), F32)
    rings = [zero] * (ROWQ - 1)
    for i in range(TAPS):
        base = jnp.broadcast_to(pats[i : i + 1, :], (XB, 128))
        rings.append(pltpu.roll(base, 0, 1, stride=1, stride_axis=0))
    rings += [zero] * ROWQ
    for kappa in range(-2, NKAP):
        pair = jnp.where(left, rings[kappa + 3], rings[kappa + 2])
        band = jnp.where(keep, jnp.concatenate([pair, pair], axis=0), 0.0)
        high = band.astype(BF16)
        rows = slice((kappa + 2) * 128, (kappa + 3) * 128)
        phigh[rows, :] = high
        plow[rows, :] = (band - high.astype(F32)).astype(BF16)


def build_planes(buf, phi, plo):
    lane = lanes(NG)

    def one(rho, carry):
        cols = [buf[j, pl.ds(rho, NG, stride=ROWQ), :] for j in range(4)]
        zero = jnp.zeros((NG, 128), F32)
        padded = [zero] + cols + [zero]
        for j in range(4):
            even = jnp.where(lane < HALF, pltpu.roll(padded[j], HALF, 1), pltpu.roll(padded[j + 1], HALF, 1))
            odd = jnp.where(
                lane < XB + HALF, pltpu.roll(padded[j + 1], XB + HALF, 1), pltpu.roll(padded[j + 2], XB + HALF, 1)
            )
            for place, part in ((2 * j, even), (2 * j + 1, odd)):
                high = part.astype(BF16).astype(F32)
                phi[rho, place] = high
                plo[rho, place] = part - high
        return carry

    lax.fori_loop(0, ROWQ, one, 0)


def convolve(steps, phi, plo, phigh, plow, acc):
    def lhs(src, a):
        return jnp.concatenate(
            [
                jnp.concatenate([src[rho, j, a + 1 : a + 1 + NQ, :].astype(BF16) for j in range(NJ)], axis=0)
                for rho in range(ROWQ)
            ],
            axis=1,
        )

    def rhs(src, a):
        return jnp.concatenate(
            [src[(a * ROWQ + 2) * 128 : (a * ROWQ + 6) * 128, :], src[a * ROWQ * 128 : (a * ROWQ + 4) * 128, :]], axis=1
        )

    def dot(x, y):
        return jnp.dot(x, y, preferred_element_type=F32)

    for a in steps:
        high, low = lhs(phi, a), lhs(plo, a)
        wide, fine = rhs(phigh, a), rhs(plow, a)
        part = dot(high, wide) + dot(low, wide) + dot(high, fine)
        if a == 0:
            acc[...] = part
        else:
            acc[...] += part


def to_matched(acc, mat, weight):
    left = lanes(NQ) < XB
    mat[0] = jnp.zeros((NROWS, 128), F32)
    mat[5] = jnp.zeros((NROWS, 128), F32)
    for j in range(4):
        for pair in range(2):
            cols = slice(pair * 128, pair * 128 + 128)
            even = acc[2 * j * NQ : (2 * j + 1) * NQ, cols] * weight
            odd = acc[(2 * j + 1) * NQ : (2 * j + 2) * NQ, cols] * weight
            mat[j + 1, pl.ds(2 * pair, NQ, stride=ROWQ), :] = jnp.where(left, even, pltpu.roll(odd, XB, 1))
            mat[j + 1, pl.ds(2 * pair + 1, NQ, stride=ROWQ), :] = jnp.where(left, pltpu.roll(even, XB, 1), odd)


def cut_tiles(offs_ref, mat, tiles):
    lane = lanes(TR)
    tiles[NTILES] = jnp.zeros((TR, 128), F32)

    def one(t, carry):
        rows = pl.ds(pl.multiple_of(t * TR, TR), TR)
        for q in range(4):
            off = offs_ref[0, t * 4 + q]
            side = jnp.where(off >= SHIFT, q + 2, q)
            turn = (128 + SHIFT - off) % 128
            own = pltpu.roll(mat[q + 1, rows, :], turn, 1)
            other = pltpu.roll(mat[side, rows, :], turn, 1)
            source = lane + (off - SHIFT)
            tiles[t * 4 + q] = jnp.where((source >= 0) & (source < 128), own, other)
        return carry

    lax.fori_loop(0, NROWS // TR, one, 0)


def kernel(
    nz, npatch,
    offs_hbm, cell_hbm, coef_hbm, wgt_hbm, row_hbm, col_hbm, img_hbm, out_ref,
    offs, cell, coef, wgt, rowt, colt,
    buf, scaled, phigh, plow, phi, plo, acc, mat, tiles,
    slotv, slots, denx, denz, send, recv_x, xsum, recv_z,
    load_sem, slot_sem, halo_send, halo_recv, denx_send, denx_recv, denz_send, denz_recv,
    x_send, x_recv, z_send, z_recv, x_token, z_token,
):
    span = nz // NCHUNK
    me, patch = lax.axis_index("exp"), lax.axis_index("patch")
    zpos, xpos = me // NX, me % NX
    barrier = pltpu.get_barrier_semaphore()

    def along_x(n):
        return (zpos * NX + (xpos + n) % NX, patch)

    def at_z(z):
        return (z * NX + xpos, patch)

    def remote(src, dst, ssem, rsem, target):
        return pltpu.make_async_remote_copy(
            src_ref=src, dst_ref=dst, send_sem=ssem, recv_sem=rsem, device_id=target, device_id_type=MESH
        )

    def signal(sem, target):
        pl.semaphore_signal(sem, inc=1, device_id=target, device_id_type=MESH)

    def halo(way):
        source, target = ((NROWS, 0), (PAD, PAD + NROWS))[way]
        return remote(
            buf.at[:, pl.ds(source, PAD), :],
            buf.at[:, pl.ds(target, PAD), :],
            halo_send.at[way],
            halo_recv.at[way],
            (me, patch + (1, -1)[way]),
        )

    def den_x(n):
        return remote(denx.at[0], denx.at[n], denx_send.at[n], denx_recv.at[n], along_x(n))

    def den_z(z, slot):
        return remote(denz.at[nz], denz.at[slot], denz_send.at[z], denz_recv.at[slot], at_z(z))

    def cells_x(n, g):
        rows = pl.ds(g * span, span)
        return remote(
            send.at[(xpos + n) % NX, rows], recv_x.at[n - 1, rows], x_send.at[n - 1, g], x_recv.at[n - 1, g], along_x(n)
        )

    def cells_z(z, slot):
        return remote(xsum.at[z], recv_z.at[slot], z_send.at[z], z_recv.at[slot], at_z(z))

    def others(action, start=0, stop=None):
        def one(z, carry):
            @pl.when(z != zpos)
            def _():
                action(z)

            return carry

        lax.fori_loop(start, nz if stop is None else stop, one, 0)

    def around(action):
        def one(d, carry):
            action((zpos + d) % nz)
            action((zpos + nz - d) % nz)
            return carry

        lax.fori_loop(1, nz // 2, one, 0)
        action((zpos + nz // 2) % nz)

    pairs = ((offs_hbm, offs), (cell_hbm, cell), (coef_hbm, coef), (wgt_hbm, wgt), (row_hbm, rowt), (col_hbm, colt))
    loads = [pltpu.make_async_copy(src, dst, load_sem.at[4 + k]) for k, (src, dst) in enumerate(pairs)]
    bands = [
        pltpu.make_async_copy(
            img_hbm.at[:, pl.ds(j * 128, 128)], buf.at[j, pl.ds(PAD, NROWS), :], load_sem.at[j]
        )
        for j in range(4)
    ]
    for copy in loads + bands:
        copy.start()

    upper, lower = patch > 0, patch < npatch - 1

    @pl.when(upper)
    def _():
        signal(barrier, (me, patch - 1))

    @pl.when(lower)
    def _():
        signal(barrier, (me, patch + 1))

    for n in (1, NX - 1):
        signal(barrier, along_x(n))
    for d in (1, nz - 1):
        signal(barrier, at_z((zpos + d) % nz))

    for copy in loads:
        copy.wait()
    build_weights(coef, rowt, colt, scaled, phigh, plow)

    lane = lanes(8)
    first = jnp.full((8, 128), NTILES, jnp.int32)
    last = jnp.full((8, 128), -1, jnp.int32)
    count = jnp.zeros((8, 128), F32)
    for k in range(NTILES):
        hit = lane == cell[0, k]
        count = count + jnp.where(hit, 1.0, 0.0)
        first = jnp.minimum(first, jnp.where(hit, k, NTILES))
        last = jnp.maximum(last, jnp.where(hit, k, -1))
    sub = lax.broadcasted_iota(jnp.int32, (8, 128), 0)
    slotv[...] = jnp.where(sub == 0, first, jnp.where(last > first, last, NTILES))
    slot_copy = pltpu.make_async_copy(slotv, slots, slot_sem)
    slot_copy.start()
    denx[0] = (count * wgt[0])[0:1]

    pl.semaphore_wait(barrier, jnp.where(upper, 1, 0) + jnp.where(lower, 1, 0) + 4)
    for copy in bands:
        copy.wait()

    @pl.when(lower)
    def _():
        halo(0).start()

    @pl.when(upper)
    def _():
        halo(1).start()

    for n in (1, NX - 1):
        signal(x_token, along_x(n))
    reach = 1
    rounds = []
    while reach < nz // 2:
        rounds.append(reach)
        reach *= 2

    def greet(r):
        for d in (rounds[r], nz - rounds[r]):
            signal(z_token.at[r], at_z((zpos + d) % nz))

    greet(0)

    @pl.when(jnp.logical_not(upper))
    def _():
        buf[:, 0:PAD, :] = jnp.zeros((4, PAD, 128), F32)

    @pl.when(jnp.logical_not(lower))
    def _():
        buf[:, PAD + NROWS : PAD + NROWS + PAD, :] = jnp.zeros((4, PAD, 128), F32)

    buf[:, PAD + NROWS + PAD :, :] = jnp.zeros((4, NG * ROWQ - NROWS - 2 * PAD, 128), F32)

    @pl.when(upper)
    def _():
        halo(0).wait_recv()

    @pl.when(lower)
    def _():
        halo(1).wait_recv()

    build_planes(buf, phi, plo)
    pl.semaphore_wait(x_token, 2)
    for n in range(1, NX):
        den_x(n).start()
    done = 0
    for r in range(1, len(rounds)):
        pl.semaphore_wait(z_token.at[r - 1], 2)
        greet(r)
        convolve(range(done, done + 4), phi, plo, phigh, plow, acc)
        done += 4
    convolve(range(done, NA), phi, plo, phigh, plow, acc)
    to_matched(acc, mat, wgt[0])
    cut_tiles(offs, mat, tiles)
    slot_copy.wait()

    def gather(depth, carry):
        for x in range(NX):
            place = depth * NX + x
            send[x, depth] = tiles[slots[0, place]] + tiles[slots[1, place]]
        return carry

    for g in range(NCHUNK):
        lax.fori_loop(g * span, (g + 1) * span, gather, 0)
        for n in (2, 1, 3):
            cells_x(n, g).start()

    pl.semaphore_wait(z_token.at[len(rounds) - 1], 2)
    for n in range(1, NX):
        den_x(n).wait_recv()
    denz[nz] = denx[0] + denx[1] + denx[2] + denx[3]
    others(lambda z: den_z(z, zpos).start())

    for g in range(NCHUNK):
        for n in range(1, NX):
            cells_x(n, g).wait_recv()
        rows = pl.ds(g * span, span)
        xsum[rows] = (send[xpos, rows] + recv_x[0, rows]) + (recv_x[1, rows] + recv_x[2, rows])
        others(lambda z: cells_z(z, zpos).start(), g * span, (g + 1) * span)

    around(lambda z: den_z(z, z).wait_recv())
    denz[zpos] = denz[nz]
    den = denz[0]
    for z in range(1, nz):
        den = den + denz[z]
    den = jnp.sum(jnp.where(lanes(1) == me, den, 0.0), axis=1, keepdims=True)
    out_ref[...] = xsum[zpos]

    def add(z):
        cells_z(z, z).wait_recv()
        out_ref[...] += recv_z[z]

    around(add)
    out_ref[...] = out_ref[...] / den

    @pl.when(lower)
    def _():
        halo(0).wait_send()

    @pl.when(upper)
    def _():
        halo(1).wait_send()

    for n in range(1, NX):
        den_x(n).wait_send()
        for g in range(NCHUNK):
            cells_x(n, g).wait_send()
    others(lambda z: den_z(z, zpos).wait_send())
    others(lambda z: cells_z(z, zpos).wait_send())


def per_device(nz, npatch, image, row_taps, col_taps, coefficients, exposure_weight, warp_offset, target_cell):
    hbm = pl.BlockSpec(memory_space=pltpu.HBM)
    vmem = pltpu.VMEM
    smem = pltpu.SMEM
    dma = pltpu.SemaphoreType.DMA
    rounds = max(1, (nz // 2 - 1).bit_length())
    out = pl.pallas_call(
        functools.partial(kernel, nz, npatch),
        out_shape=jax.ShapeDtypeStruct((TR, TW), F32),
        in_specs=[hbm] * 7,
        out_specs=pl.BlockSpec(memory_space=vmem),
        scratch_shapes=[
            smem((1, NTILES), jnp.int32),
            smem((1, NTILES), jnp.int32),
            smem((1, NB), F32),
            smem((1,), F32),
            vmem((NB, TAPS), F32),
            vmem((NB, TAPS), F32),
            vmem((4, NG * ROWQ, 128), F32),
            vmem((NB, TAPS), F32),
            vmem(((NKAP + 2) * 128, 128), BF16),
            vmem(((NKAP + 2) * 128, 128), BF16),
            vmem((ROWQ, NJ, NG, 128), F32),
            vmem((ROWQ, NJ, NG, 128), F32),
            vmem((NJ * NQ, 256), F32),
            vmem((6, NROWS, 128), F32),
            vmem((NTILES + 1, TR, TW), F32),
            vmem((8, 128), jnp.int32),
            smem((8, 128), jnp.int32),
            vmem((NX, 1, 128), F32),
            vmem((nz + 1, 1, 128), F32),
            vmem((NX, nz, TR, TW), F32),
            vmem((NX - 1, nz, TR, TW), F32),
            vmem((nz, TR, TW), F32),
            vmem((nz, TR, TW), F32),
            dma((10,)),
            dma,
            dma((2,)),
            dma((2,)),
            dma((NX,)),
            dma((NX,)),
            dma((nz,)),
            dma((nz,)),
            dma((NX - 1, NCHUNK)),
            dma((NX - 1, NCHUNK)),
            dma((nz,)),
            dma((nz,)),
            pltpu.SemaphoreType.REGULAR,
            pltpu.SemaphoreType.REGULAR((rounds,)),
        ],
        compiler_params=pltpu.CompilerParams(
            collective_id=0, has_side_effects=True, vmem_limit_bytes=60 * 2**20
        ),
    )(
        warp_offset.reshape(1, NTILES),
        target_cell.reshape(1, NTILES),
        coefficients,
        exposure_weight,
        row_taps,
        col_taps,
        image.reshape(NROWS, NCOLS),
    )
    return out[None, None]


def solution(mesh):
    nz = mesh.shape["exp"] // NX
    npatch = mesh.shape["patch"]
    return jax.shard_map(
        functools.partial(per_device, nz, npatch),
        mesh=mesh,
        in_specs=(
            P("exp", "patch", None),
            P(),
            P(),
            P("exp", None),
            P("exp"),
            P("exp", "patch", None),
            P("exp", "patch", None, None),
        ),
        out_specs=P("patch", "exp", None, None),
        check_vma=False,
    )
```

time: 45.4 us -> 36.6 us (0.81)
  Pallas kernels: 40.9 us -> 34.4 us
  local copies, waits for them, and re-layouts: 3.63 us -> 1.3 us
    pallas_call x1, Pallas kernels: 40.9 us -> 34.4 us  [per_device(): pl.pallas_call(functools.partial(kernel, nz, npatch), out_shape=jax.Shape...]
    unnamed x13 -> x1, local copies, waits for them, and re-layouts: 3.63 us -> 1.3 us
where the time goes in v2:
time: 36.6 us; the launch traced here: 36.4 us
  Pallas kernels  34.4 us (94%)
  local copies, waits for them, and re-layouts  1.3 us (4%)
  between operations  0.66 us (2%)
    pallas_call x1, Pallas kernels, per_device(): pl.pallas_call(functools.partial(kernel, nz, npatch), out_shape=jax.Shape...  34.4 us
    unnamed x1, local copies, waits for them, and re-layouts  1.3 us

profile of v2, /device:TPU:1, one launch (start us, length us, event | category | flops | bytes accessed | tf_op | source)
XLA Modules:
  0.0 36.4 jit_solution(15957489058104636506)
XLA Ops:
  0.7 34.4 %shard_map.73 = f32[16,128]{1,0:T(8,128)} custom-call(s32[1,32]{1,0:T(1,128)} %bitcast.6, s32[1,32]{1,0:T(1,128)} %bitcast.7, f32[1,20]{1,0:T(1,128)} %coef_hbm.1, f32[1]{0:T(128)S(6)} %copy.9.wgt_hbm, f32[20,41]{1,0:T(8,128)} %row_hbm.1, f32[20,41]{1,0:T(8,128)} %col_hbm.1, f32[128,512]{1,0:T(8,128)} %bitcast.4), custom_call_target="tpu_custom_call" | custom-call | tf_op jit(solution)/shard_map/pallas_call | solution.py:384
  35.1 1.3 %copy.10 = f32[1,1,16,128]{3,2,1,0:T(8,128)} copy(f32[1,1,16,128]{3,2,1,0:T(8,128)} %bitcast.5) | data formatting | bytes 16384

commit v3 on v2

--- a/solution.py
+++ b/solution.py
@@ -28,7 +28,14 @@
 NKAP = NA * ROWQ
 NQ = NROWS // ROWQ
 NG = 48
-NCHUNK = 4
+EDGE = 16
+EARLY, MID, LATE = 1, 5, 9
+AHEAD = 2
+BOUNDS = (0, 2, 5, 10, 16)
+
+
+def chunk_bounds(nz):
+    return tuple(sorted({0, nz} | {max(1, nz * step // 16) for step in BOUNDS[1:]}))
 
 
 def lanes(rows):
@@ -63,12 +70,11 @@
         plow[rows, :] = (band - high.astype(F32)).astype(BF16)
 
 
-def build_planes(buf, phi, plo):
-    lane = lanes(NG)
-
-    def one(rho, carry):
-        cols = [buf[j, pl.ds(rho, NG, stride=ROWQ), :] for j in range(4)]
-        zero = jnp.zeros((NG, 128), F32)
+def build_planes(groups, buf, phi, plo):
+    lane = lanes(groups)
+    zero = jnp.zeros((groups, 128), F32)
+    for rho in range(ROWQ):
+        cols = [buf[j, pl.ds(rho, groups, stride=ROWQ), :] for j in range(4)]
         padded = [zero] + cols + [zero]
         for j in range(4):
             even = jnp.where(lane < HALF, pltpu.roll(padded[j], HALF, 1), pltpu.roll(padded[j + 1], HALF, 1))
@@ -79,22 +85,19 @@
                 high = part.astype(BF16).astype(F32)
                 phi[rho, place] = high
                 plo[rho, place] = part - high
-        return carry
-
-    lax.fori_loop(0, ROWQ, one, 0)
-
-
-def convolve(steps, phi, plo, phigh, plow, acc):
-    def lhs(src, a):
+
+
+def products(a, start, rows, phi, plo, phigh, plow):
+    def lhs(src):
         return jnp.concatenate(
             [
-                jnp.concatenate([src[rho, j, a + 1 : a + 1 + NQ, :].astype(BF16) for j in range(NJ)], axis=0)
+                jnp.concatenate([src[rho, j, start : start + rows, :].astype(BF16) for j in range(NJ)], axis=0)
                 for rho in range(ROWQ)
             ],
             axis=1,
         )
 
-    def rhs(src, a):
+    def rhs(src):
         return jnp.concatenate(
             [src[(a * ROWQ + 2) * 128 : (a * ROWQ + 6) * 128, :], src[a * ROWQ * 128 : (a * ROWQ + 4) * 128, :]], axis=1
         )
@@ -102,14 +105,28 @@
     def dot(x, y):
         return jnp.dot(x, y, preferred_element_type=F32)
 
+    high, low = lhs(phi), lhs(plo)
+    wide, fine = rhs(phigh), rhs(plow)
+    return dot(high, wide) + dot(low, wide) + dot(high, fine)
+
+
+def convolve(steps, phi, plo, phigh, plow, acc):
     for a in steps:
-        high, low = lhs(phi, a), lhs(plo, a)
-        wide, fine = rhs(phigh, a), rhs(plow, a)
-        part = dot(high, wide) + dot(low, wide) + dot(high, fine)
+        part = products(a, a + 1, NQ, phi, plo, phigh, plow)
         if a == 0:
             acc[...] = part
         else:
             acc[...] += part
+
+
+def add_edges(ehi, elo, phigh, plow, acc):
+    reach = HALF // ROWQ
+    tops = [products(a, a + 1, 8, ehi, elo, phigh, plow) for a in range(reach)]
+    ends = [products(a, EDGE + a - 5, 8, ehi, elo, phigh, plow) for a in range(NA - reach, NA)]
+    for parts, row in ((tops, 0), (ends, NQ - 8)):
+        total = sum(parts[1:], parts[0])
+        for j in range(NJ):
+            acc[j * NQ + row : j * NQ + row + 8, :] += total[j * 8 : j * 8 + 8, :]
 
 
 def to_matched(acc, mat, weight):
@@ -128,32 +145,28 @@
 def cut_tiles(offs_ref, mat, tiles):
     lane = lanes(TR)
     tiles[NTILES] = jnp.zeros((TR, 128), F32)
-
-    def one(t, carry):
-        rows = pl.ds(pl.multiple_of(t * TR, TR), TR)
-        for q in range(4):
-            off = offs_ref[0, t * 4 + q]
-            side = jnp.where(off >= SHIFT, q + 2, q)
-            turn = (128 + SHIFT - off) % 128
-            own = pltpu.roll(mat[q + 1, rows, :], turn, 1)
-            other = pltpu.roll(mat[side, rows, :], turn, 1)
-            source = lane + (off - SHIFT)
-            tiles[t * 4 + q] = jnp.where((source >= 0) & (source < 128), own, other)
-        return carry
-
-    lax.fori_loop(0, NROWS // TR, one, 0)
+    for k in range(NTILES):
+        t, q = k // 4, k % 4
+        rows = slice(t * TR, t * TR + TR)
+        off = offs_ref[0, k]
+        side = jnp.where(off >= SHIFT, q + 2, q)
+        turn = (128 + SHIFT - off) % 128
+        own = pltpu.roll(mat[q + 1, rows, :], turn, 1)
+        other = pltpu.roll(mat[side, rows, :], turn, 1)
+        source = lane + (off - SHIFT)
+        tiles[k] = jnp.where((source >= 0) & (source < 128), own, other)
 
 
 def kernel(
     nz, npatch,
     offs_hbm, cell_hbm, coef_hbm, wgt_hbm, row_hbm, col_hbm, img_hbm, out_ref,
     offs, cell, coef, wgt, rowt, colt,
-    buf, scaled, phigh, plow, phi, plo, acc, mat, tiles,
+    buf, edge, scaled, phigh, plow, phi, plo, ehi, elo, acc, mat, tiles,
     slotv, slots, denx, denz, send, recv_x, xsum, recv_z,
     load_sem, slot_sem, halo_send, halo_recv, denx_send, denx_recv, denz_send, denz_recv,
     x_send, x_recv, z_send, z_recv, x_token, z_token,
 ):
-    span = nz // NCHUNK
+    bounds = chunk_bounds(nz)
     me, patch = lax.axis_index("exp"), lax.axis_index("patch")
     zpos, xpos = me // NX, me % NX
     barrier = pltpu.get_barrier_semaphore()
@@ -173,10 +186,10 @@
         pl.semaphore_signal(sem, inc=1, device_id=target, device_id_type=MESH)
 
     def halo(way):
-        source, target = ((NROWS, 0), (PAD, PAD + NROWS))[way]
+        source, target = ((NROWS, 0), (PAD, (EDGE + 8) * ROWQ))[way]
         return remote(
             buf.at[:, pl.ds(source, PAD), :],
-            buf.at[:, pl.ds(target, PAD), :],
+            edge.at[:, pl.ds(target, PAD), :],
             halo_send.at[way],
             halo_recv.at[way],
             (me, patch + (1, -1)[way]),
@@ -189,7 +202,7 @@
         return remote(denz.at[nz], denz.at[slot], denz_send.at[z], denz_recv.at[slot], at_z(z))
 
     def cells_x(n, g):
-        rows = pl.ds(g * span, span)
+        rows = pl.ds(bounds[g], bounds[g + 1] - bounds[g])
         return remote(
             send.at[(xpos + n) % NX, rows], recv_x.at[n - 1, rows], x_send.at[n - 1, g], x_recv.at[n - 1, g], along_x(n)
         )
@@ -261,9 +274,26 @@
     slot_copy.start()
     denx[0] = (count * wgt[0])[0:1]
 
-    pl.semaphore_wait(barrier, jnp.where(upper, 1, 0) + jnp.where(lower, 1, 0) + 4)
+    buf[:, 0:PAD, :] = jnp.zeros((4, PAD, 128), F32)
+    buf[:, PAD + NROWS :, :] = jnp.zeros((4, NG * ROWQ - NROWS - PAD, 128), F32)
+    top, end = slice(0, PAD), slice((EDGE + 8) * ROWQ, (EDGE + 8) * ROWQ + PAD)
+    edge[:, PAD : end.start, :] = jnp.zeros((4, end.start - PAD, 128), F32)
+    edge[:, end.stop :, :] = jnp.zeros((4, 2 * EDGE * ROWQ - end.stop, 128), F32)
+
+    @pl.when(jnp.logical_not(upper))
+    def _():
+        edge[:, top, :] = jnp.zeros((4, PAD, 128), F32)
+
+    @pl.when(jnp.logical_not(lower))
+    def _():
+        edge[:, end, :] = jnp.zeros((4, PAD, 128), F32)
+
     for copy in bands:
         copy.wait()
+    build_planes(NG, buf, phi, plo)
+    convolve(range(0, EARLY), phi, plo, phigh, plow, acc)
+
+    pl.semaphore_wait(barrier, jnp.where(upper, 1, 0) + jnp.where(lower, 1, 0) + 4)
 
     @pl.when(lower)
     def _():
@@ -275,27 +305,23 @@
 
     for n in (1, NX - 1):
         signal(x_token, along_x(n))
-    reach = 1
-    rounds = []
-    while reach < nz // 2:
-        rounds.append(reach)
-        reach *= 2
+    rounds = [1 << r for r in range(max(1, (nz // 2 - 1).bit_length()))]
 
     def greet(r):
         for d in (rounds[r], nz - rounds[r]):
             signal(z_token.at[r], at_z((zpos + d) % nz))
 
     greet(0)
-
-    @pl.when(jnp.logical_not(upper))
-    def _():
-        buf[:, 0:PAD, :] = jnp.zeros((4, PAD, 128), F32)
-
-    @pl.when(jnp.logical_not(lower))
-    def _():
-        buf[:, PAD + NROWS : PAD + NROWS + PAD, :] = jnp.zeros((4, PAD, 128), F32)
-
-    buf[:, PAD + NROWS + PAD :, :] = jnp.zeros((4, NG * ROWQ - NROWS - 2 * PAD, 128), F32)
+    stops = [EARLY, MID, LATE][: len(rounds)] + [NA]
+    for r in range(len(rounds)):
+        convolve(range(stops[r], stops[r + 1]), phi, plo, phigh, plow, acc)
+        if r + 1 < len(rounds):
+            pl.semaphore_wait(z_token.at[r], 2)
+            greet(r + 1)
+        if r == 0:
+            pl.semaphore_wait(x_token, 2)
+            for n in range(1, NX):
+                den_x(n).start()
 
     @pl.when(upper)
     def _():
@@ -305,44 +331,38 @@
     def _():
         halo(1).wait_recv()
 
-    build_planes(buf, phi, plo)
-    pl.semaphore_wait(x_token, 2)
-    for n in range(1, NX):
-        den_x(n).start()
-    done = 0
-    for r in range(1, len(rounds)):
-        pl.semaphore_wait(z_token.at[r - 1], 2)
-        greet(r)
-        convolve(range(done, done + 4), phi, plo, phigh, plow, acc)
-        done += 4
-    convolve(range(done, NA), phi, plo, phigh, plow, acc)
+    build_planes(2 * EDGE, edge, ehi, elo)
+    add_edges(ehi, elo, phigh, plow, acc)
     to_matched(acc, mat, wgt[0])
     cut_tiles(offs, mat, tiles)
     slot_copy.wait()
 
-    def gather(depth, carry):
-        for x in range(NX):
-            place = depth * NX + x
-            send[x, depth] = tiles[slots[0, place]] + tiles[slots[1, place]]
-        return carry
-
-    for g in range(NCHUNK):
-        lax.fori_loop(g * span, (g + 1) * span, gather, 0)
+    groups = len(bounds) - 1
+
+    def send_x(g):
+        for depth in range(bounds[g], bounds[g + 1]):
+            for x in range(NX):
+                place = depth * NX + x
+                send[x, depth] = tiles[slots[0, place]] + tiles[slots[1, place]]
         for n in (2, 1, 3):
             cells_x(n, g).start()
 
+    for g in range(min(AHEAD, groups)):
+        send_x(g)
     pl.semaphore_wait(z_token.at[len(rounds) - 1], 2)
     for n in range(1, NX):
         den_x(n).wait_recv()
     denz[nz] = denx[0] + denx[1] + denx[2] + denx[3]
     others(lambda z: den_z(z, zpos).start())
 
-    for g in range(NCHUNK):
+    for g in range(groups):
         for n in range(1, NX):
             cells_x(n, g).wait_recv()
-        rows = pl.ds(g * span, span)
+        rows = pl.ds(bounds[g], bounds[g + 1] - bounds[g])
         xsum[rows] = (send[xpos, rows] + recv_x[0, rows]) + (recv_x[1, rows] + recv_x[2, rows])
-        others(lambda z: cells_z(z, zpos).start(), g * span, (g + 1) * span)
+        others(lambda z: cells_z(z, zpos).start(), bounds[g], bounds[g + 1])
+        if g + AHEAD < groups:
+            send_x(g + AHEAD)
 
     around(lambda z: den_z(z, z).wait_recv())
     denz[zpos] = denz[nz]
@@ -369,7 +389,7 @@
 
     for n in range(1, NX):
         den_x(n).wait_send()
-        for g in range(NCHUNK):
+        for g in range(len(bounds) - 1):
             cells_x(n, g).wait_send()
     others(lambda z: den_z(z, zpos).wait_send())
     others(lambda z: cells_z(z, zpos).wait_send())
@@ -394,11 +414,14 @@
             vmem((NB, TAPS), F32),
             vmem((NB, TAPS), F32),
             vmem((4, NG * ROWQ, 128), F32),
+            vmem((4, 2 * EDGE * ROWQ, 128), F32),
             vmem((NB, TAPS), F32),
             vmem(((NKAP + 2) * 128, 128), BF16),
             vmem(((NKAP + 2) * 128, 128), BF16),
             vmem((ROWQ, NJ, NG, 128), F32),
             vmem((ROWQ, NJ, NG, 128), F32),
+            vmem((ROWQ, NJ, 2 * EDGE, 128), F32),
+            vmem((ROWQ, NJ, 2 * EDGE, 128), F32),
             vmem((NJ * NQ, 256), F32),
             vmem((6, NROWS, 128), F32),
             vmem((NTILES + 1, TR, TW), F32),
@@ -418,24 +441,29 @@
             dma((NX,)),
             dma((nz,)),
             dma((nz,)),
-            dma((NX - 1, NCHUNK)),
-            dma((NX - 1, NCHUNK)),
+            dma((NX - 1, len(chunk_bounds(nz)) - 1)),
+            dma((NX - 1, len(chunk_bounds(nz)) - 1)),
             dma((nz,)),
             dma((nz,)),
             pltpu.SemaphoreType.REGULAR,
             pltpu.SemaphoreType.REGULAR((rounds,)),
         ],
         compiler_params=pltpu.CompilerParams(
-            collective_id=0, has_side_effects=True, vmem_limit_bytes=60 * 2**20
+            collective_id=0, has_side_effects=True, vmem_limit_bytes=48 * 2**20
         ),
     )(
-        warp_offset.reshape(1, NTILES),
-        target_cell.reshape(1, NTILES),
-        coefficients,
-        exposure_weight,
-        row_taps,
-        col_taps,
-        image.reshape(NROWS, NCOLS),
+        *(
+            part if part.size == 1 else pltpu.with_memory_space_constraint(part, pltpu.HBM)
+            for part in (
+                warp_offset.reshape(1, NTILES),
+                target_cell.reshape(1, NTILES),
+                coefficients,
+                exposure_weight,
+                row_taps,
+                col_taps,
+                image.reshape(NROWS, NCOLS),
+            )
+        )
     )
     return out[None, None]
 

time: 36.6 us -> 32.7 us (0.89)
  the two profiles are of different devices: /device:TPU:1 before, /device:TPU:16 now
where the time goes in v3:
time: 32.7 us; the launch traced here: 32.6 us
  Pallas kernels  31.3 us (96%)
  between operations  0.66 us (2%)
  local copies, waits for them, and re-layouts  0.6 us (2%)
    pallas_call x1, Pallas kernels, per_device(): pl.pallas_call(functools.partial(kernel, nz, npatch), out_shape=jax.Shape...  31.3 us

profile of v3, /device:TPU:16, one launch (start us, length us, event | category | flops | bytes accessed | tf_op | source)
XLA Modules:
  0.0 32.6 jit_solution(8494846265390573765)
XLA Ops:
  0.7 31.3 %shard_map.73 = f32[16,128]{1,0:T(8,128)S(1)} custom-call(s32[1,32]{1,0:T(1,128)} %bitcast.6, s32[1,32]{1,0:T(1,128)} %bitcast.7, f32[1,20]{1,0:T(1,128)} %coef_hbm.1, f32[1]{0:T(128)S(6)} %copy.9.wgt_hbm, f32[20,41]{1,0:T(8,128)} %row_hbm.1, f32[20,41]{1,0:T(8,128)} %col_hbm.1, f32[128,512]{1,0:T(8,128)} %bitcast.5), custom_call_target="tpu_custom_call" | custom-call | tf_op jit(solution)/shard_map/pallas_call | solution.py:404
  32.0 0.6 %copy.10 = f32[1,1,16,128]{3,2,1,0:T(8,128)} copy(f32[1,1,16,128]{3,2,1,0:T(8,128)S(1)} %bitcast.4) | data formatting | bytes 16384

commit v4 on v3

--- a/solution.py
+++ b/solution.py
@@ -29,8 +29,8 @@
 NQ = NROWS // ROWQ
 NG = 48
 EDGE = 16
-EARLY, MID, LATE = 1, 5, 9
-AHEAD = 2
+MID, LATE = 5, 11
+AHEAD = 9
 BOUNDS = (0, 2, 5, 10, 16)
 
 
@@ -70,7 +70,7 @@
         plow[rows, :] = (band - high.astype(F32)).astype(BF16)
 
 
-def build_planes(groups, buf, phi, plo):
+def build_planes(groups, base, buf, phi, plo):
     lane = lanes(groups)
     zero = jnp.zeros((groups, 128), F32)
     for rho in range(ROWQ):
@@ -83,8 +83,8 @@
             )
             for place, part in ((2 * j, even), (2 * j + 1, odd)):
                 high = part.astype(BF16).astype(F32)
-                phi[rho, place] = high
-                plo[rho, place] = part - high
+                phi[rho, place, base : base + groups, :] = high
+                plo[rho, place, base : base + groups, :] = part - high
 
 
 def products(a, start, rows, phi, plo, phigh, plow):
@@ -106,8 +106,8 @@
         return jnp.dot(x, y, preferred_element_type=F32)
 
     high, low = lhs(phi), lhs(plo)
-    wide, fine = rhs(phigh), rhs(plow)
-    return dot(high, wide) + dot(low, wide) + dot(high, fine)
+    both = dot(jnp.concatenate([high, low], axis=0), rhs(phigh))
+    return both[: NJ * rows] + both[NJ * rows :] + dot(high, rhs(plow))
 
 
 def convolve(steps, phi, plo, phigh, plow, acc):
@@ -121,8 +121,8 @@
 
 def add_edges(ehi, elo, phigh, plow, acc):
     reach = HALF // ROWQ
-    tops = [products(a, a + 1, 8, ehi, elo, phigh, plow) for a in range(reach)]
-    ends = [products(a, EDGE + a - 5, 8, ehi, elo, phigh, plow) for a in range(NA - reach, NA)]
+    tops = [products(a, EDGE + a + 1, 8, ehi, elo, phigh, plow) for a in range(reach)]
+    ends = [products(a, a - 5, 8, ehi, elo, phigh, plow) for a in range(NA - reach, NA)]
     for parts, row in ((tops, 0), (ends, NQ - 8)):
         total = sum(parts[1:], parts[0])
         for j in range(NJ):
@@ -186,7 +186,7 @@
         pl.semaphore_signal(sem, inc=1, device_id=target, device_id_type=MESH)
 
     def halo(way):
-        source, target = ((NROWS, 0), (PAD, (EDGE + 8) * ROWQ))[way]
+        source, target = ((NROWS, 8 * ROWQ), (PAD, 0))[way]
         return remote(
             buf.at[:, pl.ds(source, PAD), :],
             edge.at[:, pl.ds(target, PAD), :],
@@ -259,6 +259,45 @@
         copy.wait()
     build_weights(coef, rowt, colt, scaled, phigh, plow)
 
+    for copy in bands:
+        copy.wait()
+    pl.semaphore_wait(barrier, jnp.where(upper, 1, 0) + jnp.where(lower, 1, 0) + 4)
+
+    @pl.when(lower)
+    def _():
+        halo(0).start()
+
+    @pl.when(upper)
+    def _():
+        halo(1).start()
+
+    for n in (1, NX - 1):
+        signal(x_token, along_x(n))
+    rounds = [1 << r for r in range(max(1, (nz // 2 - 1).bit_length()))]
+
+    def greet(r):
+        for d in (rounds[r], nz - rounds[r]):
+            signal(z_token.at[r], at_z((zpos + d) % nz))
+
+    greet(0)
+    buf[:, 0:PAD, :] = jnp.zeros((4, PAD, 128), F32)
+    buf[:, PAD + NROWS :, :] = jnp.zeros((4, NG * ROWQ - NROWS - PAD, 128), F32)
+    gap = jnp.zeros((4, 8, 128), F32)
+    edge[:, PAD : PAD + 8, :] = gap
+    edge[:, EDGE * ROWQ - 8 :, :] = gap
+    for plane in (ehi, elo):
+        plane[:, :, 0:8, :] = jnp.zeros((ROWQ, NJ, 8, 128), F32)
+        plane[:, :, EDGE + 8 :, :] = jnp.zeros((ROWQ, NJ, 8, 128), F32)
+
+    @pl.when(jnp.logical_not(upper))
+    def _():
+        edge[:, 8 * ROWQ : 8 * ROWQ + PAD, :] = jnp.zeros((4, PAD, 128), F32)
+
+    @pl.when(jnp.logical_not(lower))
+    def _():
+        edge[:, 0:PAD, :] = jnp.zeros((4, PAD, 128), F32)
+
+    build_planes(NG, 0, buf, phi, plo)
     lane = lanes(8)
     first = jnp.full((8, 128), NTILES, jnp.int32)
     last = jnp.full((8, 128), -1, jnp.int32)
@@ -274,45 +313,7 @@
     slot_copy.start()
     denx[0] = (count * wgt[0])[0:1]
 
-    buf[:, 0:PAD, :] = jnp.zeros((4, PAD, 128), F32)
-    buf[:, PAD + NROWS :, :] = jnp.zeros((4, NG * ROWQ - NROWS - PAD, 128), F32)
-    top, end = slice(0, PAD), slice((EDGE + 8) * ROWQ, (EDGE + 8) * ROWQ + PAD)
-    edge[:, PAD : end.start, :] = jnp.zeros((4, end.start - PAD, 128), F32)
-    edge[:, end.stop :, :] = jnp.zeros((4, 2 * EDGE * ROWQ - end.stop, 128), F32)
-
-    @pl.when(jnp.logical_not(upper))
-    def _():
-        edge[:, top, :] = jnp.zeros((4, PAD, 128), F32)
-
-    @pl.when(jnp.logical_not(lower))
-    def _():
-        edge[:, end, :] = jnp.zeros((4, PAD, 128), F32)
-
-    for copy in bands:
-        copy.wait()
-    build_planes(NG, buf, phi, plo)
-    convolve(range(0, EARLY), phi, plo, phigh, plow, acc)
-
-    pl.semaphore_wait(barrier, jnp.where(upper, 1, 0) + jnp.where(lower, 1, 0) + 4)
-
-    @pl.when(lower)
-    def _():
-        halo(0).start()
-
-    @pl.when(upper)
-    def _():
-        halo(1).start()
-
-    for n in (1, NX - 1):
-        signal(x_token, along_x(n))
-    rounds = [1 << r for r in range(max(1, (nz // 2 - 1).bit_length()))]
-
-    def greet(r):
-        for d in (rounds[r], nz - rounds[r]):
-            signal(z_token.at[r], at_z((zpos + d) % nz))
-
-    greet(0)
-    stops = [EARLY, MID, LATE][: len(rounds)] + [NA]
+    stops = [0, MID, LATE][: len(rounds)] + [NA]
     for r in range(len(rounds)):
         convolve(range(stops[r], stops[r + 1]), phi, plo, phigh, plow, acc)
         if r + 1 < len(rounds):
@@ -331,7 +332,7 @@
     def _():
         halo(1).wait_recv()
 
-    build_planes(2 * EDGE, edge, ehi, elo)
+    build_planes(EDGE, 8, edge, ehi, elo)
     add_edges(ehi, elo, phigh, plow, acc)
     to_matched(acc, mat, wgt[0])
     cut_tiles(offs, mat, tiles)
@@ -414,7 +415,7 @@
             vmem((NB, TAPS), F32),
             vmem((NB, TAPS), F32),
             vmem((4, NG * ROWQ, 128), F32),
-            vmem((4, 2 * EDGE * ROWQ, 128), F32),
+            vmem((4, EDGE * ROWQ, 128), F32),
             vmem((NB, TAPS), F32),
             vmem(((NKAP + 2) * 128, 128), BF16),
             vmem(((NKAP + 2) * 128, 128), BF16),

time: 32.7 us -> 31.7 us (0.969)
  the two profiles are of different devices: /device:TPU:16 before, /device:TPU:1 now
where the time goes in v4:
time: 31.7 us; the launch traced here: 31.1 us
  Pallas kernels  29.8 us (94%)
  between operations  0.66 us (2%)
  local copies, waits for them, and re-layouts  0.6 us (2%)
    pallas_call x1, Pallas kernels, per_device(): pl.pallas_call(functools.partial(kernel, nz, npatch), out_shape=jax.Shape...  29.8 us

profile of v4, /device:TPU:1, one launch (start us, length us, event | category | flops | bytes accessed | tf_op | source)
XLA Modules:
  0.0 31.1 jit_solution(11716353780104215095)
XLA Ops:
  0.7 29.8 %shard_map.73 = f32[16,128]{1,0:T(8,128)S(1)} custom-call(s32[1,32]{1,0:T(1,128)} %bitcast.6, s32[1,32]{1,0:T(1,128)} %bitcast.7, f32[1,20]{1,0:T(1,128)} %coef_hbm.1, f32[1]{0:T(128)S(6)} %copy.9.wgt_hbm, f32[20,41]{1,0:T(8,128)} %row_hbm.1, f32[20,41]{1,0:T(8,128)} %col_hbm.1, f32[128,512]{1,0:T(8,128)} %bitcast.5), custom_call_target="tpu_custom_call" | custom-call | tf_op jit(solution)/shard_map/pallas_call | solution.py:405
  30.4 0.6 %copy.10 = f32[1,1,16,128]{3,2,1,0:T(8,128)} copy(f32[1,1,16,128]{3,2,1,0:T(8,128)S(1)} %bitcast.4) | data formatting | bytes 16384

commit v5 on v4

--- a/solution.py
+++ b/solution.py
@@ -29,9 +29,10 @@
 NQ = NROWS // ROWQ
 NG = 48
 EDGE = 16
-MID, LATE = 5, 11
+MID = 5
+RELAY = (1, 4, 1)
 AHEAD = 9
-BOUNDS = (0, 2, 5, 10, 16)
+BOUNDS = (0, 1, 2, 4, 6, 8, 10, 12, 14, 16)
 
 
 def chunk_bounds(nz):
@@ -73,18 +74,18 @@
 def build_planes(groups, base, buf, phi, plo):
     lane = lanes(groups)
     zero = jnp.zeros((groups, 128), F32)
+    rows = slice(base, base + groups)
     for rho in range(ROWQ):
         cols = [buf[j, pl.ds(rho, groups, stride=ROWQ), :] for j in range(4)]
-        padded = [zero] + cols + [zero]
+        near = [zero] + [pltpu.roll(part, HALF, 1) for part in cols]
+        far = [pltpu.roll(part, XB + HALF, 1) for part in cols] + [zero]
         for j in range(4):
-            even = jnp.where(lane < HALF, pltpu.roll(padded[j], HALF, 1), pltpu.roll(padded[j + 1], HALF, 1))
-            odd = jnp.where(
-                lane < XB + HALF, pltpu.roll(padded[j + 1], XB + HALF, 1), pltpu.roll(padded[j + 2], XB + HALF, 1)
-            )
+            even = jnp.where(lane < HALF, near[j], near[j + 1])
+            odd = jnp.where(lane < XB + HALF, far[j], far[j + 1])
             for place, part in ((2 * j, even), (2 * j + 1, odd)):
                 high = part.astype(BF16).astype(F32)
-                phi[rho, place, base : base + groups, :] = high
-                plo[rho, place, base : base + groups, :] = part - high
+                phi[rho, place, rows, :] = high
+                plo[rho, place, rows, :] = part - high
 
 
 def products(a, start, rows, phi, plo, phigh, plow):
@@ -112,7 +113,7 @@
 
 def convolve(steps, phi, plo, phigh, plow, acc):
     for a in steps:
-        part = products(a, a + 1, NQ, phi, plo, phigh, plow)
+        part = products(a, a + 3, NQ, phi, plo, phigh, plow)
         if a == 0:
             acc[...] = part
         else:
@@ -131,8 +132,6 @@
 
 def to_matched(acc, mat, weight):
     left = lanes(NQ) < XB
-    mat[0] = jnp.zeros((NROWS, 128), F32)
-    mat[5] = jnp.zeros((NROWS, 128), F32)
     for j in range(4):
         for pair in range(2):
             cols = slice(pair * 128, pair * 128 + 128)
@@ -144,7 +143,6 @@
 
 def cut_tiles(offs_ref, mat, tiles):
     lane = lanes(TR)
-    tiles[NTILES] = jnp.zeros((TR, 128), F32)
     for k in range(NTILES):
         t, q = k // 4, k % 4
         rows = slice(t * TR, t * TR + TR)
@@ -186,7 +184,7 @@
         pl.semaphore_signal(sem, inc=1, device_id=target, device_id_type=MESH)
 
     def halo(way):
-        source, target = ((NROWS, 8 * ROWQ), (PAD, 0))[way]
+        source, target = ((NROWS - PAD, 8 * ROWQ), (0, 0))[way]
         return remote(
             buf.at[:, pl.ds(source, PAD), :],
             edge.at[:, pl.ds(target, PAD), :],
@@ -233,7 +231,7 @@
     loads = [pltpu.make_async_copy(src, dst, load_sem.at[4 + k]) for k, (src, dst) in enumerate(pairs)]
     bands = [
         pltpu.make_async_copy(
-            img_hbm.at[:, pl.ds(j * 128, 128)], buf.at[j, pl.ds(PAD, NROWS), :], load_sem.at[j]
+            img_hbm.at[:, pl.ds(j * 128, 128)], buf.at[j], load_sem.at[j]
         )
         for j in range(4)
     ]
@@ -255,6 +253,25 @@
     for d in (1, nz - 1):
         signal(barrier, at_z((zpos + d) % nz))
 
+    gap = jnp.zeros((4, 8, 128), F32)
+    edge[:, PAD : PAD + 8, :] = gap
+    edge[:, EDGE * ROWQ - 8 :, :] = gap
+    blank = jnp.zeros((ROWQ, NJ, 8, 128), F32)
+    for plane, live in ((phi, NQ), (plo, NQ), (ehi, EDGE), (elo, EDGE)):
+        plane[:, :, 0:8, :] = blank
+        plane[:, :, live + 8 :, :] = blank
+    mat[0] = jnp.zeros((NROWS, 128), F32)
+    mat[5] = jnp.zeros((NROWS, 128), F32)
+    tiles[NTILES] = jnp.zeros((TR, 128), F32)
+
+    @pl.when(jnp.logical_not(upper))
+    def _():
+        edge[:, 8 * ROWQ : 8 * ROWQ + PAD, :] = jnp.zeros((4, PAD, 128), F32)
+
+    @pl.when(jnp.logical_not(lower))
+    def _():
+        edge[:, 0:PAD, :] = jnp.zeros((4, PAD, 128), F32)
+
     for copy in loads:
         copy.wait()
     build_weights(coef, rowt, colt, scaled, phigh, plow)
@@ -280,24 +297,7 @@
             signal(z_token.at[r], at_z((zpos + d) % nz))
 
     greet(0)
-    buf[:, 0:PAD, :] = jnp.zeros((4, PAD, 128), F32)
-    buf[:, PAD + NROWS :, :] = jnp.zeros((4, NG * ROWQ - NROWS - PAD, 128), F32)
-    gap = jnp.zeros((4, 8, 128), F32)
-    edge[:, PAD : PAD + 8, :] = gap
-    edge[:, EDGE * ROWQ - 8 :, :] = gap
-    for plane in (ehi, elo):
-        plane[:, :, 0:8, :] = jnp.zeros((ROWQ, NJ, 8, 128), F32)
-        plane[:, :, EDGE + 8 :, :] = jnp.zeros((ROWQ, NJ, 8, 128), F32)
-
-    @pl.when(jnp.logical_not(upper))
-    def _():
-        edge[:, 8 * ROWQ : 8 * ROWQ + PAD, :] = jnp.zeros((4, PAD, 128), F32)
-
-    @pl.when(jnp.logical_not(lower))
-    def _():
-        edge[:, 0:PAD, :] = jnp.zeros((4, PAD, 128), F32)
-
-    build_planes(NG, 0, buf, phi, plo)
+    build_planes(NQ, 8, buf, phi, plo)
     lane = lanes(8)
     first = jnp.full((8, 128), NTILES, jnp.int32)
     last = jnp.full((8, 128), -1, jnp.int32)
@@ -313,17 +313,21 @@
     slot_copy.start()
     denx[0] = (count * wgt[0])[0:1]
 
-    stops = [0, MID, LATE][: len(rounds)] + [NA]
-    for r in range(len(rounds)):
-        convolve(range(stops[r], stops[r + 1]), phi, plo, phigh, plow, acc)
-        if r + 1 < len(rounds):
-            pl.semaphore_wait(z_token.at[r], 2)
-            greet(r + 1)
-        if r == 0:
+    def relay(place):
+        for r in range(1, len(rounds)):
+            if RELAY[r - 1] == place:
+                pl.semaphore_wait(z_token.at[r - 1], 2)
+                greet(r)
+        if RELAY[2] == place:
             pl.semaphore_wait(x_token, 2)
             for n in range(1, NX):
                 den_x(n).start()
 
+    convolve(range(0, MID), phi, plo, phigh, plow, acc)
+    relay(0)
+    convolve(range(MID, NA), phi, plo, phigh, plow, acc)
+    relay(1)
+
     @pl.when(upper)
     def _():
         halo(0).wait_recv()
@@ -332,8 +336,10 @@
     def _():
         halo(1).wait_recv()
 
+    relay(2)
     build_planes(EDGE, 8, edge, ehi, elo)
     add_edges(ehi, elo, phigh, plow, acc)
+    relay(3)
     to_matched(acc, mat, wgt[0])
     cut_tiles(offs, mat, tiles)
     slot_copy.wait()
@@ -350,6 +356,7 @@
 
     for g in range(min(AHEAD, groups)):
         send_x(g)
+    relay(4)
     pl.semaphore_wait(z_token.at[len(rounds) - 1], 2)
     for n in range(1, NX):
         den_x(n).wait_recv()
@@ -371,15 +378,6 @@
     for z in range(1, nz):
         den = den + denz[z]
     den = jnp.sum(jnp.where(lanes(1) == me, den, 0.0), axis=1, keepdims=True)
-    out_ref[...] = xsum[zpos]
-
-    def add(z):
-        cells_z(z, z).wait_recv()
-        out_ref[...] += recv_z[z]
-
-    around(add)
-    out_ref[...] = out_ref[...] / den
-
     @pl.when(lower)
     def _():
         halo(0).wait_send()
@@ -392,6 +390,16 @@
         den_x(n).wait_send()
         for g in range(len(bounds) - 1):
             cells_x(n, g).wait_send()
+
+    out_ref[...] = xsum[zpos]
+
+    def add(z):
+        cells_z(z, z).wait_recv()
+        out_ref[...] += recv_z[z]
+
+    around(add)
+    out_ref[...] = out_ref[...] / den
+
     others(lambda z: den_z(z, zpos).wait_send())
     others(lambda z: cells_z(z, zpos).wait_send())
 
@@ -414,7 +422,7 @@
             smem((1,), F32),
             vmem((NB, TAPS), F32),
             vmem((NB, TAPS), F32),
-            vmem((4, NG * ROWQ, 128), F32),
+            vmem((4, NROWS, 128), F32),
             vmem((4, EDGE * ROWQ, 128), F32),
             vmem((NB, TAPS), F32),
             vmem(((NKAP + 2) * 128, 128), BF16),

time: 31.7 us -> 31 us (0.978)
  the two profiles are of different devices: /device:TPU:1 before, /device:TPU:32 now
where the time goes in v5:
time: 31 us; the launch traced here: 30.8 us
  Pallas kernels  29.6 us (95%)
  between operations  0.66 us (2%)
  local copies, waits for them, and re-layouts  0.6 us (2%)
    pallas_call x1, Pallas kernels, per_device(): pl.pallas_call(functools.partial(kernel, nz, npatch), out_shape=jax.Shape...  29.6 us

profile of v5, /device:TPU:32, one launch (start us, length us, event | category | flops | bytes accessed | tf_op | source)
XLA Modules:
  0.0 30.8 jit_solution(2324736177745447617)
XLA Ops:
  0.7 29.6 %shard_map.73 = f32[16,128]{1,0:T(8,128)S(1)} custom-call(s32[1,32]{1,0:T(1,128)} %bitcast.6, s32[1,32]{1,0:T(1,128)} %bitcast.7, f32[1,20]{1,0:T(1,128)} %coef_hbm.1, f32[1]{0:T(128)S(6)} %copy.9.wgt_hbm, f32[20,41]{1,0:T(8,128)} %row_hbm.1, f32[20,41]{1,0:T(8,128)} %col_hbm.1, f32[128,512]{1,0:T(8,128)} %bitcast.5), custom_call_target="tpu_custom_call" | custom-call | tf_op jit(solution)/shard_map/pallas_call | solution.py:413
  30.2 0.6 %copy.10 = f32[1,1,16,128]{3,2,1,0:T(8,128)} copy(f32[1,1,16,128]{3,2,1,0:T(8,128)S(1)} %bitcast.4) | data formatting | bytes 16384

commit v6 on v5

--- a/solution.py
+++ b/solution.py
@@ -231,7 +231,7 @@
     loads = [pltpu.make_async_copy(src, dst, load_sem.at[4 + k]) for k, (src, dst) in enumerate(pairs)]
     bands = [
         pltpu.make_async_copy(
-            img_hbm.at[:, pl.ds(j * 128, 128)], buf.at[j], load_sem.at[j]
+            img_hbm.at[:, pl.ds(j * 128, 128)], buf.at[j, pl.ds(0, NROWS), :], load_sem.at[j]
         )
         for j in range(4)
     ]
@@ -255,13 +255,13 @@
 
     gap = jnp.zeros((4, 8, 128), F32)
     edge[:, PAD : PAD + 8, :] = gap
-    edge[:, EDGE * ROWQ - 8 :, :] = gap
+    edge[:, EDGE * ROWQ - 8 : EDGE * ROWQ, :] = gap
     blank = jnp.zeros((ROWQ, NJ, 8, 128), F32)
     for plane, live in ((phi, NQ), (plo, NQ), (ehi, EDGE), (elo, EDGE)):
         plane[:, :, 0:8, :] = blank
         plane[:, :, live + 8 :, :] = blank
-    mat[0] = jnp.zeros((NROWS, 128), F32)
-    mat[5] = jnp.zeros((NROWS, 128), F32)
+    mat[0, 0:NROWS, :] = jnp.zeros((NROWS, 128), F32)
+    mat[5, 0:NROWS, :] = jnp.zeros((NROWS, 128), F32)
     tiles[NTILES] = jnp.zeros((TR, 128), F32)
 
     @pl.when(jnp.logical_not(upper))
@@ -422,8 +422,8 @@
             smem((1,), F32),
             vmem((NB, TAPS), F32),
             vmem((NB, TAPS), F32),
-            vmem((4, NROWS, 128), F32),
-            vmem((4, EDGE * ROWQ, 128), F32),
+            vmem((4, NROWS + 8, 128), F32),
+            vmem((4, EDGE * ROWQ + 8, 128), F32),
             vmem((NB, TAPS), F32),
             vmem(((NKAP + 2) * 128, 128), BF16),
             vmem(((NKAP + 2) * 128, 128), BF16),
@@ -432,7 +432,7 @@
             vmem((ROWQ, NJ, 2 * EDGE, 128), F32),
             vmem((ROWQ, NJ, 2 * EDGE, 128), F32),
             vmem((NJ * NQ, 256), F32),
-            vmem((6, NROWS, 128), F32),
+            vmem((6, NROWS + 8, 128), F32),
             vmem((NTILES + 1, TR, TW), F32),
             vmem((8, 128), jnp.int32),
             smem((8, 128), jnp.int32),

time: 31 us -> 31 us (level)
  no operation moved by 1% of the time
where the time goes in v6:
time: 31 us; the launch traced here: 30.8 us
  Pallas kernels  29.6 us (95%)
  between operations  0.66 us (2%)
  local copies, waits for them, and re-layouts  0.6 us (2%)
    pallas_call x1, Pallas kernels, per_device(): pl.pallas_call(functools.partial(kernel, nz, npatch), out_shape=jax.Shape...  29.6 us

profile of v6, /device:TPU:32, one launch (start us, length us, event | category | flops | bytes accessed | tf_op | source)
XLA Modules:
  0.0 30.8 jit_solution(9453139546246118158)
XLA Ops:
  0.7 29.6 %shard_map.73 = f32[16,128]{1,0:T(8,128)S(1)} custom-call(s32[1,32]{1,0:T(1,128)} %bitcast.6, s32[1,32]{1,0:T(1,128)} %bitcast.7, f32[1,20]{1,0:T(1,128)} %coef_hbm.1, f32[1]{0:T(128)S(6)} %copy.9.wgt_hbm, f32[20,41]{1,0:T(8,128)} %row_hbm.1, f32[20,41]{1,0:T(8,128)} %col_hbm.1, f32[128,512]{1,0:T(8,128)} %bitcast.5), custom_call_target="tpu_custom_call" | custom-call | tf_op jit(solution)/shard_map/pallas_call | solution.py:413
  30.2 0.6 %copy.10 = f32[1,1,16,128]{3,2,1,0:T(8,128)} copy(f32[1,1,16,128]{3,2,1,0:T(8,128)S(1)} %bitcast.4) | data formatting | bytes 16384
